TPU v7x, 512 devices: a whole 4x8x8 slice. The times are simulated.
512 devices in a mesh: ctx: 64 (over x, z, core), tp: 8 (over y).
Axes of the slice: x: 4, y: 8, z: 8, core: 2. Of those that a mesh axis runs over, the one named last changes fastest.
Arguments:
- features: bfloat16 [128, 196, 1152], P('ctx', None, 'tp'), may hold values from -6 to 6
- group_kernel: bfloat16 [9, 1152, 48], P(None, 'tp'), may hold values from -0.3125 to 0.3125
- squeeze_in: bfloat16 [1152, 288], P('tp'), may hold values from -0.75 to 0.75
- squeeze_out: bfloat16 [288, 1152], P(None, 'tp'), may hold values from -0.75 to 0.75
- sampler_kernel: bfloat16 [1152, 8, 1152], P('ctx', None, 'tp'), may hold values from -0.0625 to 0.0625
- readout_kernel: bfloat16 [1152, 8192], P('ctx', 'tp'), may hold values from -0.1875 to 0.1875
- frame_clip: int32 [128], replicated, may hold values from 0 to 15, as said below
- clip_keep: int32 [16], replicated, may hold values from 1 to 512, as said below
- token_cotangent: bfloat16 [4096, 8192], P('ctx', 'tp'), may hold values from -6 to 6
Outputs:
- llm_tokens: bfloat16 [4096, 8192], P('ctx', 'tp')
- grad_features: bfloat16 [128, 196, 1152], P('ctx', None, 'tp')
Inputs may be any that keep to these rules, and one draw needn't show every extreme that they name: `frame_clip`: clip ids start at 0 and never fall along the frames; every clip covers an even number of frames from 2 to 16 and starts at an even frame; some clip covers 16. `clip_keep`: each clip keeps at least one and at most 8 * 8 times half its frames of its tokens; the clip of 16 frames keeps all of its tokens, and some clip keeps a single token.
All inputs are finite; a program needn't handle non-finite values.
Results may differ from a plain program's by a relative error of at most 0.009.
Values may be sent and summed in bfloat16 or wider, within the bound.
A program may use at most 64 MiB of HBM per device.

v0:
```python
import jax
import jax.numpy as jnp
from jax import lax
from jax.sharding import PartitionSpec as P

SIDE = 14
OUT_SIDE = 8


def shifted(value, axis, by):
    count = lax.axis_size(axis)
    pairs = [(i, i + by) for i in range(count) if 0 <= i + by < count]
    return lax.ppermute(value, axis, pairs)


def silu_slope(values):
    sigma = jax.nn.sigmoid(values)
    return sigma * (1.0 + values * (1.0 - sigma))


def grouped_forward(frames_grid, group_kernel):
    count, side, _, chans = frames_grid.shape
    width = group_kernel.shape[2]
    groups = chans // width
    padded = jnp.pad(frames_grid, ((0, 0), (1, 1), (1, 1), (0, 0)))
    kernel = group_kernel.reshape(9, groups, width, width)
    total = jnp.zeros((count, side, side, groups, width), jnp.float32)
    for kernel_tap in range(9):
        row_shift, col_shift = divmod(kernel_tap, 3)
        window = padded[:, row_shift : row_shift + side, col_shift : col_shift + side]
        window = window.reshape(count, side, side, groups, width)
        total = total + jnp.einsum(
            "fyxgi,gio->fyxgo", window, kernel[kernel_tap], preferred_element_type=jnp.float32
        )
    return total.reshape(count, side, side, chans)


def grouped_backward(grad_grid, group_kernel):
    count, side, _, chans = grad_grid.shape
    width = group_kernel.shape[2]
    groups = chans // width
    kernel = group_kernel.reshape(9, groups, width, width)
    source = grad_grid.reshape(count, side, side, groups, width)
    total = jnp.zeros((count, side + 2, side + 2, chans), jnp.float32)
    for kernel_tap in range(9):
        row_shift, col_shift = divmod(kernel_tap, 3)
        spread = jnp.einsum(
            "fyxgo,gio->fyxgi", source, kernel[kernel_tap], preferred_element_type=jnp.float32
        )
        spread = spread.reshape(count, side, side, chans)
        total = total + jnp.pad(
            spread, ((0, 0), (row_shift, 2 - row_shift), (col_shift, 2 - col_shift), (0, 0))
        )
    return total[:, 1 : side + 1, 1 : side + 1]


def make_patches(prev_odd, even):
    stacked = jnp.stack([prev_odd, even], axis=1)
    stacked = jnp.pad(stacked, ((0, 0), (0, 0), (1, 1), (1, 1), (0, 0)))
    pairs, _, padded_side, _, chans = stacked.shape
    half = padded_side // 2
    shaped = stacked.reshape(pairs, 2, half, 2, half, 2, chans).transpose(0, 2, 4, 1, 3, 5, 6)
    return shaped.reshape(pairs * half * half, 8 * chans)


def unpatch(grad_rows, pairs, side, chans):
    half = side // 2 + 1
    shaped = grad_rows.reshape(pairs, half, half, 2, 2, 2, chans).transpose(0, 3, 1, 4, 2, 5, 6)
    shaped = shaped.reshape(pairs, 2, 2 * half, 2 * half, chans)
    return shaped[:, :, 1 : side + 1, 1 : side + 1]


def contract_last(left, right):
    return lax.dot_general(
        left, right, (((1,), (1,)), ((), ())), preferred_element_type=jnp.float32
    )


def per_device(
    features,
    group_kernel,
    squeeze_in,
    squeeze_out,
    sampler_kernel,
    readout_kernel,
    frame_clip,
    clip_keep,
    token_cotangent,
):
    highest = lax.Precision.HIGHEST
    shard_index = lax.axis_index("ctx")
    frames_dev, cells, chans = features.shape
    pairs_dev = frames_dev // 2
    grid = features.reshape(frames_dev, SIDE, SIDE, chans)
    conv_out = grouped_forward(grid, group_kernel)
    active = jax.nn.silu(conv_out)
    pooled = jnp.mean(active, axis=(1, 2))
    squeezed = lax.psum(jnp.dot(pooled, squeeze_in.astype(jnp.float32), precision=highest), "tp")
    relaxed = jax.nn.silu(squeezed)
    excite = jax.nn.sigmoid(jnp.dot(relaxed, squeeze_out.astype(jnp.float32), precision=highest))
    hidden = (grid.astype(jnp.float32) + active * excite[:, None, None, :]).astype(jnp.bfloat16)
    full_sampler, full_readout = (
        lax.all_gather(sampler_kernel, "ctx", axis=0, tiled=True),
        lax.all_gather(readout_kernel, "ctx", axis=0, tiled=True),
    )
    sampler_rows = full_sampler.reshape(full_sampler.shape[0], 8 * chans)
    halo_frame = shifted(hidden[-1], "ctx", 1)
    local_clip = lax.dynamic_slice_in_dim(frame_clip, shard_index * frames_dev, frames_dev)
    edge_clip = lax.dynamic_slice_in_dim(
        frame_clip, jnp.maximum(shard_index * frames_dev - 1, 0), 1
    )
    first_keep = jnp.logical_and(shard_index > 0, edge_clip[0] == local_clip[0])
    later_keep = local_clip[1:-1:2] == local_clip[2::2]
    pair_mask = jnp.concatenate([first_keep[None], later_keep]).astype(jnp.float32)
    even = hidden[0::2]
    odd = hidden[1::2]
    prev_odd = jnp.concatenate([halo_frame[None], odd[:-1]], axis=0)
    prev_odd = prev_odd * pair_mask.astype(jnp.bfloat16)[:, None, None, None]
    patches = make_patches(prev_odd, even)
    per_frame = OUT_SIDE * OUT_SIDE
    pair_clip = frame_clip[0::2]
    clip_ids = jnp.arange(clip_keep.shape[0], dtype=jnp.int32)
    start_pair = jnp.sum((pair_clip[None, :] < clip_ids[:, None]).astype(jnp.int32), axis=1)
    own_clip = local_clip[0::2]
    one_hot = (own_clip[:, None] == clip_ids[None, :]).astype(jnp.int32)
    own_start = jnp.sum(one_hot * start_pair[None, :], axis=1)
    own_keep = jnp.sum(one_hot * clip_keep[None, :], axis=1)
    pair_index = shard_index * pairs_dev + jnp.arange(pairs_dev, dtype=jnp.int32)
    position = (pair_index - own_start)[:, None] * per_frame + jnp.arange(
        per_frame, dtype=jnp.int32
    )[None, :]
    live = (position < own_keep[:, None]).reshape(-1).astype(jnp.bfloat16)
    pre = lax.psum(contract_last(patches, sampler_rows), "tp")
    act = jax.nn.silu(pre).astype(jnp.bfloat16)
    tokens = (
        jnp.dot(act, full_readout, preferred_element_type=jnp.float32).astype(jnp.bfloat16)
        * live[:, None]
    )
    llm_tokens = lax.all_to_all(tokens, "ctx", split_axis=0, concat_axis=0, tiled=True)
    back = (
        lax.all_to_all(token_cotangent, "ctx", split_axis=0, concat_axis=0, tiled=True)
        * live[:, None]
    )
    grad_act = lax.psum(contract_last(back, full_readout), "tp")
    grad_pre = (grad_act * silu_slope(pre)).astype(jnp.bfloat16)
    grad_patches = jnp.dot(grad_pre, sampler_rows, preferred_element_type=jnp.float32)
    grad_taps = unpatch(grad_patches, pairs_dev, SIDE, chans)
    leading = grad_taps[:, 0] * pair_mask[:, None, None, None]
    incoming = shifted(leading[0].astype(jnp.bfloat16), "ctx", -1).astype(jnp.float32)
    grad_even = grad_taps[:, 1]
    grad_odd = jnp.concatenate([leading[1:], incoming[None]], axis=0)
    grad_hidden = jnp.stack([grad_even, grad_odd], axis=1).reshape(frames_dev, SIDE, SIDE, chans)
    grad_excite = jnp.sum(grad_hidden * active, axis=(1, 2))
    grad_inner = grad_excite * excite * (1.0 - excite)
    grad_relaxed = lax.psum(
        jnp.dot(grad_inner, squeeze_out.astype(jnp.float32).T, precision=highest), "tp"
    )
    grad_squeezed = grad_relaxed * silu_slope(squeezed)
    grad_pooled = jnp.dot(grad_squeezed, squeeze_in.astype(jnp.float32).T, precision=highest)
    grad_active = grad_hidden * excite[:, None, None, :] + grad_pooled[:, None, None, :] / cells
    grad_conv = (grad_active * silu_slope(conv_out)).astype(jnp.bfloat16)
    grad_grid = grad_hidden + grouped_backward(grad_conv, group_kernel)
    grad_features = grad_grid.astype(jnp.bfloat16).reshape(frames_dev, cells, chans)
    return (llm_tokens, grad_features)


def solution(mesh):
    placed = (
        P("ctx", None, "tp"),
        P(None, "tp", None),
        P("tp", None),
        P(None, "tp"),
        P("ctx", None, "tp"),
        P("ctx", "tp"),
        P(),
        P(),
        P("ctx", "tp"),
    )
    return jax.shard_map(
        per_device,
        mesh=mesh,
        in_specs=placed,
        out_specs=(P("ctx", "tp"), P("ctx", None, "tp")),
        check_vma=False,
    )
```

profile of v0, /device:TPU:1, one launch (start us, length us, event | category | flops | bytes accessed | tf_op | source)
XLA Modules:
  0.0 345.6 jit_solution(8308310035529797624)
XLA Ops:
  10.8 1.5 fusion.52
  12.4 2.3 pad_slice_fusion
  19.0 2.0 reshape.192
  21.2 2.0 reshape.193
  27.1 14.9 %psum.28 = f32[2,288]{1,0:T(2,128)S(1)} all-reduce(f32[2,288]{1,0:T(2,128)S(1)} %fusion.54), channel_id=1, replica_groups=mesh['ctx'=64,'tp'=8] {'tp'}, use_global_device_ids=true, to_apply=%region_1.2 | all-reduce | flops 576 | bytes 4608 | tf_op jit(solution)/shard_map/psum | solution.py:98
  42.8 1.4 add_convert_fusion
  44.5 8.1 %collective-permute-start = (bf16[14,14,144]{2,1,0:T(8,128)(2,1)S(1)}, bf16[14,14,144]{2,1,0:T(8,128)(2,1)S(1)}, u32[]{:S(2)}, u32[]{:S(2)}) collective-permute-start(bf16[14,14,144]{2,1,0:T(8,128)(2,1)S(1)} %bitcast.239), channel_id=1, source_target_pairs={{0,8},{8,16},{16,24},{24,32},{32,40},{40,48},{48,56},{56,64},{64,7... | collective-permute-start | bytes 169352 | tf_op jit(solution)/shard_map/ppermute | solution.py:13
  54.5 12.5 %all-to-all-start.1 = ((bf16[64,2,512]{2,1,0:T(2,128)(2,1)}), bf16[64,2,512]{2,1,0:T(2,128)(2,1)S(1)}, u32[]{:S(2)}, u32[]{:S(2)}) async-start(bf16[64,2,512]{2,1,0:T(2,128)(2,1)} %reshape.225), calls=%async_computation.1 | async-start | bytes 262144 | tf_op jit(solution)/shard_map/all_to_all | solution.py:141
  73.3 4.1 %all-to-all-done.1 = bf16[64,2,512]{2,1,0:T(2,128)(2,1)S(1)} async-done(((bf16[64,2,512]{2,1,0:T(2,128)(2,1)}), bf16[64,2,512]{2,1,0:T(2,128)(2,1)S(1)}, u32[]{:S(2)}, u32[]{:S(2)}) %all-to-all-start.1) | async-done | bytes 131104 | tf_op jit(solution)/shard_map/all_to_all | solution.py:141
  77.6 24.3 %all-gather.6.cloned.1.call-done = bf16[64,18,1024]{2,1,0:T(8,128)(2,1)} async-done(((bf16[1,18,1024]{2,1,0:T(8,128)(2,1)}), bf16[64,18,1024]{2,1,0:T(8,128)(2,1)}) %all-gather.6.cloned.1.call-update) | async-done | bytes 2359312 | tf_op jit(solution)/shard_map/all_gather | solution.py:104
  101.9 2.9 reshape.212
  104.8 1.6 fusion.29
  106.4 81.2 %all-gather.4.cloned.1.call-done = bf16[1152,8,144]{2,1,0:T(8,128)(2,1)} async-done(((bf16[18,8,144]{2,1,0:T(8,128)(2,1)}), bf16[1152,8,144]{2,1,0:T(8,128)(2,1)}) %all-gather.4.cloned.1.call-update) | async-done | bytes 2654224 | tf_op jit(solution)/shard_map/all_gather | solution.py:103
  187.6 5.5 %copy.254 = bf16[1152,8,144]{0,2,1:T(8,128)(2,1)S(1)} copy(bf16[1152,8,144]{2,1,0:T(8,128)(2,1)} %all-gather.4.cloned.1.call-done) | data formatting | bytes 5308416 | tf_op jit(solution)/shard_map/all_gather | solution.py:103
  193.1 2.2 fusion.55
  195.4 71.2 %all-reduce.14.cloned.1.call-done = (f32[64,1152]{1,0:T(8,128)}, f32[64,1152]{1,0:T(8,128)}) async-done(((f32[64,1152]{1,0:T(8,128)}, f32[64,1152]{1,0:T(8,128)}), (f32[64,1152]{1,0:T(8,128)}, f32[64,1152]{1,0:T(8,128)})) %all-reduce.14.cloned.1.call-update) | async-done | bytes 589840 | tf_op jit(solution)/shard_map/psum | solution.py:144
  266.6 2.3 convolution_bitcast_fusion.14
  270.2 7.3 %collective-permute-start.1 = (bf16[14,14,144]{2,1,0:T(8,128)(2,1)S(1)}, bf16[14,14,144]{2,1,0:T(8,128)(2,1)S(1)}, u32[]{:S(2)}, u32[]{:S(2)}) collective-permute-start(bf16[14,14,144]{2,1,0:T(8,128)(2,1)S(1)} %fusion.31), channel_id=1, source_target_pairs={{8,0},{16,8},{24,16},{32,24},{40,32},{48,40},{56,48},{64,56},{72,6... | collective-permute-start | bytes 169352 | tf_op jit(solution)/shard_map/ppermute | solution.py:13
  279.6 10.5 %all-to-all-start = ((bf16[64,2,512]{2,1,0:T(2,128)(2,1)}), bf16[64,2,512]{2,1,0:T(2,128)(2,1)S(1)}, u32[]{:S(2)}, u32[]{:S(2)}) async-start(bf16[64,2,512]{2,1,0:T(2,128)(2,1)} %reshape.227), calls=%async_computation | async-start | bytes 262144 | tf_op jit(solution)/shard_map/all_to_all | solution.py:139
  290.9 13.6 %psum.31 = f32[2,288]{1,0:T(2,128)S(1)} all-reduce(f32[2,288]{1,0:T(2,128)S(1)} %fusion.39), channel_id=1, replica_groups=mesh['ctx'=64,'tp'=8] {'tp'}, use_global_device_ids=true, to_apply=%region_8.9 | all-reduce | flops 576 | bytes 4608 | tf_op jit(solution)/shard_map/psum | solution.py:155
  313.8 1.5 copy.264
  316.7 1.5 copy.265
  318.2 1.4 reshape.203
  319.6 1.5 copy.266
  322.4 1.5 copy.267
  323.9 1.4 reshape.205
  325.3 1.5 copy.268
  328.6 1.4 reshape.207
  330.4 1.4 reshape.208
  332.1 1.4 reshape.209
  333.5 1.5 pad_add_fusion
  335.1 2.4 fusion.15
  (172 shorter events, 40.1 us)
Async XLA Ops:
  7.2 35.4 %copy-start = (bf16[288,144]{0,1:T(8,128)(2,1)S(1)}, bf16[288,144]{0,1:T(8,128)(2,1)}, u32[]{:S(2)}) copy-start(bf16[288,144]{0,1:T(8,128)(2,1)} %param.12) | copy-start | bytes 248836
  7.2 94.7 %all-gather.6.cloned.1.call-start = ((), (), s32[]{:S(2)}) async-start(), calls=%async_computation.3 | async-start | bytes 3194880 | tf_op jit(solution)/shard_map/all_gather | solution.py:104
  7.9 179.7 %all-gather.4.cloned.1.call-start = ((), (), s32[]{:S(2)}) async-start(), calls=%async_computation.2 | async-start | bytes 4792320 | tf_op jit(solution)/shard_map/all_gather | solution.py:103
  15.1 8.3 %copy-start.9 = (bf16[1,144,48]{2,1,0:T(8,128)(2,1)}, bf16[1,144,48]{2,1,0:T(8,128)(2,1)S(1)}, u32[]{:S(2)}) copy-start(bf16[1,144,48]{2,1,0:T(8,128)(2,1)S(1)} %copy.233) | copy-start | bytes 41476
  15.5 8.2 %copy-start.11 = (bf16[1,144,48]{2,1,0:T(8,128)(2,1)}, bf16[1,144,48]{2,1,0:T(8,128)(2,1)S(1)}, u32[]{:S(2)}) copy-start(bf16[1,144,48]{2,1,0:T(8,128)(2,1)S(1)} %copy.235) | copy-start | bytes 41476
  15.8 8.0 %copy-start.13 = (bf16[1,144,48]{2,1,0:T(8,128)(2,1)}, bf16[1,144,48]{2,1,0:T(8,128)(2,1)S(1)}, u32[]{:S(2)}) copy-start(bf16[1,144,48]{2,1,0:T(8,128)(2,1)S(1)} %copy.237) | copy-start | bytes 41476
  16.2 7.9 %copy-start.15 = (bf16[1,144,48]{2,1,0:T(8,128)(2,1)}, bf16[1,144,48]{2,1,0:T(8,128)(2,1)S(1)}, u32[]{:S(2)}) copy-start(bf16[1,144,48]{2,1,0:T(8,128)(2,1)S(1)} %copy.239) | copy-start | bytes 41476
  16.6 7.8 %copy-start.17 = (bf16[1,144,48]{2,1,0:T(8,128)(2,1)}, bf16[1,144,48]{2,1,0:T(8,128)(2,1)S(1)}, u32[]{:S(2)}) copy-start(bf16[1,144,48]{2,1,0:T(8,128)(2,1)S(1)} %copy.242) | copy-start | bytes 41476
  16.9 7.7 %copy-start.19 = (bf16[1,144,48]{2,1,0:T(8,128)(2,1)}, bf16[1,144,48]{2,1,0:T(8,128)(2,1)S(1)}, u32[]{:S(2)}) copy-start(bf16[1,144,48]{2,1,0:T(8,128)(2,1)S(1)} %copy.244) | copy-start | bytes 41476
  19.0 5.8 %copy-start.21 = (bf16[1,144,48]{2,1,0:T(8,128)(2,1)}, bf16[1,144,48]{2,1,0:T(8,128)(2,1)S(1)}, u32[]{:S(2)}) copy-start(bf16[1,144,48]{2,1,0:T(8,128)(2,1)S(1)} %copy.246) | copy-start | bytes 41476
  21.2 4.2 %copy-start.23 = (bf16[1,144,48]{2,1,0:T(8,128)(2,1)}, bf16[1,144,48]{2,1,0:T(8,128)(2,1)S(1)}, u32[]{:S(2)}) copy-start(bf16[1,144,48]{2,1,0:T(8,128)(2,1)S(1)} %copy.248) | copy-start | bytes 41476
  25.8 27.4 %copy-start.25 = (bf16[64,1024]{1,0:T(8,128)(2,1)S(1)}, bf16[64,1024]{1,0:T(8,128)(2,1)}, u32[]{:S(2)}) copy-start(bf16[64,1024]{1,0:T(8,128)(2,1)} %param.17) | copy-start | bytes 393220
  26.3 41.0 %copy-start.33 = (s32[128]{0:T(128)S(1)}, s32[128]{0:T(128)}, u32[]{:S(2)}) copy-start(s32[128]{0:T(128)} %param.15) | copy-start | bytes 1540
  26.3 44.0 %copy-start.34 = (s32[16]{0:T(128)S(1)}, s32[16]{0:T(128)}, u32[]{:S(2)}) copy-start(s32[16]{0:T(128)} %param.16) | copy-start | bytes 196
  44.5 27.1 %collective-permute-start = (bf16[14,14,144]{2,1,0:T(8,128)(2,1)S(1)}, bf16[14,14,144]{2,1,0:T(8,128)(2,1)S(1)}, u32[]{:S(2)}, u32[]{:S(2)}) collective-permute-start(bf16[14,14,144]{2,1,0:T(8,128)(2,1)S(1)} %bitcast.239), channel_id=1, source_target_pairs={{0,8},{8,16},{16,24},{24,32},{32,40},{40,48},{48,56},{56,64},{64,7... | collective-permute-start | bytes 169352 | tf_op jit(solution)/shard_map/ppermute | solution.py:13
  54.5 22.9 %all-to-all-start.1 = ((bf16[64,2,512]{2,1,0:T(2,128)(2,1)}), bf16[64,2,512]{2,1,0:T(2,128)(2,1)S(1)}, u32[]{:S(2)}, u32[]{:S(2)}) async-start(bf16[64,2,512]{2,1,0:T(2,128)(2,1)} %reshape.225), calls=%async_computation.1 | async-start | bytes 262144 | tf_op jit(solution)/shard_map/all_to_all | solution.py:141
  67.1 199.5 %all-reduce.14.cloned.1.call-start = ((), (), s32[]{:S(2)}) async-start(), calls=%async_computation.4 | async-start | bytes 1179648 | tf_op jit(solution)/shard_map/psum | solution.py:144
  71.6 33.2 %copy-start.30 = (bf16[64]{0:T(256)(128)(2,1)}, bf16[64]{0:T(256)(128)(2,1)S(1)}, u32[]{:S(2)}) copy-start(bf16[64]{0:T(256)(128)(2,1)S(1)} %compare_convert_fusion) | copy-start | bytes 388
  266.6 10.8 %copy-start.2 = (bf16[1152,1024]{1,0:T(8,128)(2,1)S(1)}, bf16[1152,1024]{1,0:T(8,128)(2,1)}, u32[]{:S(2)}) copy-start(bf16[1152,1024]{1,0:T(8,128)(2,1)} %copy-done.1) | copy-start | bytes 7077892
  266.6 10.8 %copy-start.31 = (bf16[64]{0:T(256)(128)(2,1)S(1)}, bf16[64]{0:T(256)(128)(2,1)}, u32[]{:S(2)}) copy-start(bf16[64]{0:T(256)(128)(2,1)} %copy-done.30) | copy-start | bytes 388
  266.6 10.8 %copy-start.32 = (f32[64,1152]{1,0:T(8,128)S(1)}, f32[64,1152]{1,0:T(8,128)}, u32[]{:S(2)}) copy-start(f32[64,1152]{1,0:T(8,128)} %get-tuple-element.15) | copy-start | bytes 884740
  270.1 20.1 %copy-start.3 = (f32[2,14,14,144]{3,0,2,1:T(2,128)S(1)}, f32[2,14,14,144]{3,0,2,1:T(2,128)}, u32[]{:S(2)}) copy-start(f32[2,14,14,144]{3,0,2,1:T(2,128)} %get-tuple-element.17) | copy-start | bytes 677380
  270.1 34.4 %copy-start.27 = (bf16[144,288]{1,0:T(8,128)(2,1)S(1)}, bf16[144,288]{1,0:T(8,128)(2,1)}, u32[]{:S(2)}) copy-start(bf16[144,288]{1,0:T(8,128)(2,1)} %param.11) | copy-start | bytes 248836
  270.1 34.4 %copy-start.29 = (f32[2,288]{1,0:T(2,128)S(1)}, f32[2,288]{1,0:T(2,128)}, u32[]{:S(2)}) copy-start(f32[2,288]{1,0:T(2,128)} %copy-done.28) | copy-start | bytes 6916
  270.2 20.0 %collective-permute-start.1 = (bf16[14,14,144]{2,1,0:T(8,128)(2,1)S(1)}, bf16[14,14,144]{2,1,0:T(8,128)(2,1)S(1)}, u32[]{:S(2)}, u32[]{:S(2)}) collective-permute-start(bf16[14,14,144]{2,1,0:T(8,128)(2,1)S(1)} %fusion.31), channel_id=1, source_target_pairs={{8,0},{16,8},{24,16},{32,24},{40,32},{48,40},{56,48},{64,56},{72,6... | collective-permute-start | bytes 169352 | tf_op jit(solution)/shard_map/ppermute | solution.py:13
  279.6 58.6 %all-to-all-start = ((bf16[64,2,512]{2,1,0:T(2,128)(2,1)}), bf16[64,2,512]{2,1,0:T(2,128)(2,1)S(1)}, u32[]{:S(2)}, u32[]{:S(2)}) async-start(bf16[64,2,512]{2,1,0:T(2,128)(2,1)} %reshape.227), calls=%async_computation | async-start | bytes 262144 | tf_op jit(solution)/shard_map/all_to_all | solution.py:139
  290.1 15.6 %copy-start.10 = (bf16[1,144,48]{2,1,0:T(8,128)(2,1)S(1)}, bf16[1,144,48]{2,1,0:T(8,128)(2,1)}, u32[]{:S(2)}) copy-start(bf16[1,144,48]{2,1,0:T(8,128)(2,1)} %copy-done.9) | copy-start | bytes 41476
  290.9 15.9 %copy-start.12 = (bf16[1,144,48]{2,1,0:T(8,128)(2,1)S(1)}, bf16[1,144,48]{2,1,0:T(8,128)(2,1)}, u32[]{:S(2)}) copy-start(bf16[1,144,48]{2,1,0:T(8,128)(2,1)} %copy-done.11) | copy-start | bytes 41476
  305.2 3.9 %copy-start.16 = (bf16[1,144,48]{2,1,0:T(8,128)(2,1)S(1)}, bf16[1,144,48]{2,1,0:T(8,128)(2,1)}, u32[]{:S(2)}) copy-start(bf16[1,144,48]{2,1,0:T(8,128)(2,1)} %copy-done.15) | copy-start | bytes 41476
  305.5 4.7 %copy-start.18 = (bf16[1,144,48]{2,1,0:T(8,128)(2,1)S(1)}, bf16[1,144,48]{2,1,0:T(8,128)(2,1)}, u32[]{:S(2)}) copy-start(bf16[1,144,48]{2,1,0:T(8,128)(2,1)} %copy-done.17) | copy-start | bytes 41476
  305.8 5.5 %copy-start.20 = (bf16[1,144,48]{2,1,0:T(8,128)(2,1)S(1)}, bf16[1,144,48]{2,1,0:T(8,128)(2,1)}, u32[]{:S(2)}) copy-start(bf16[1,144,48]{2,1,0:T(8,128)(2,1)} %copy-done.19) | copy-start | bytes 41476
  306.9 4.7 %copy-start.22 = (bf16[1,144,48]{2,1,0:T(8,128)(2,1)S(1)}, bf16[1,144,48]{2,1,0:T(8,128)(2,1)}, u32[]{:S(2)}) copy-start(bf16[1,144,48]{2,1,0:T(8,128)(2,1)} %copy-done.21) | copy-start | bytes 41476
  (10 other events, 22.3 us)
Sparse Core Ops, SparseCore 0:
  11.3 90.4 all-gather.5
  105.2 82.3 all-gather.3
  195.5 71.1 all-reduce.13
where the time goes:
time: 349 us; the launch traced here: 346 us
  waiting for transfers between devices  182 us (52%)
  local copies, waits for them, and re-layouts  54.8 us (16%)
  starting transfers between devices  38.7 us (11%)
  blocking collectives  28.5 us (8%)
  matrix products  16 us (5%)
  between operations  15.9 us (5%)
  other arithmetic  9.6 us (3%)
    all_gather x1, waiting for transfers between devices, per_device(): lax.all_gather(sampler_kernel, 'ctx', axis=0, tiled=True)  81.2 us
    psum x1, waiting for transfers between devices, per_device(): grad_act = lax.psum(contract_last(back, full_readout), 'tp')  71.2 us
    all_gather x1, waiting for transfers between devices, per_device(): lax.all_gather(readout_kernel, 'ctx', axis=0, tiled=True)  24.3 us
    ppermute x2, starting transfers between devices, shifted(): return lax.ppermute(value, axis, pairs)  15.4 us
    psum x1, blocking collectives, per_device(): lax.psum(jnp.dot(pooled, squeeze_in.astype(jnp.float32), precision=highes...  14.9 us
    psum x1, blocking collectives, per_device(): lax.psum(jnp.dot(grad_inner, squeeze_out.astype(jnp.float32).T, precision...  13.6 us
    all_to_all x1, starting transfers between devices, per_device(): lax.all_to_all(token_cotangent, 'ctx', split_axis=0, concat_axis=0, tiled...  12.5 us
    reshape x9, local copies, waits for them, and re-layouts, grouped_backward(): spread = spread.reshape(count, side, side, chans)  12.2 us
  transfers between devices with their start and end apart: 7, of which 4 were waited for; matrix products, arithmetic and copies ran while one was open for 19% of the time, Pallas kernels for 0%

commit v1 on v0

v1 whole, which is shorter than its diff:
```python
import jax
import jax.numpy as jnp
from jax import lax
from jax.experimental import pallas as pl
from jax.experimental.pallas import tpu as pltpu
from jax.sharding import PartitionSpec as P

NX, NZ, NT = 4, 8, 8
BF = jnp.bfloat16
F32 = jnp.float32
MESH = pl.DeviceIdType.MESH
SLOT = (0, 128, 256, 384, 640, 768, 896, 1024)


def iota(shape, dim):
    return lax.broadcasted_iota(jnp.int32, shape, dim)


def select(hit):
    return jnp.where(hit, 1.0, 0.0).astype(BF)


def mm(a, b):
    return jnp.dot(a, b, preferred_element_type=F32)


def mmt(a, b):
    return lax.dot_general(a, b, (((1,), (1,)), ((), ())), preferred_element_type=F32)


def exact(dot, value, weight):
    high = value.astype(BF)
    left = value - high.astype(F32)
    middle = left.astype(BF)
    low = (left - middle.astype(F32)).astype(BF)
    return dot(high, weight) + (dot(middle, weight) + dot(low, weight))


def sigmoid(v):
    return jax.nn.sigmoid(v)


def slope(v):
    s = sigmoid(v)
    return s * (1.0 + v * (1.0 - s))


def padded_place(cell):
    row = (cell * 4682) >> 16
    return (row + 1) * 16 + (cell - 14 * row) + 1


def patch_place(r):
    s = r >> 6
    a = (r >> 3) & 7
    b = r & 7
    return (2 * a + (s >> 1)) * 16 + 2 * b + (s & 1)


def third(v):
    return (v >= 48).astype(jnp.int32) + (v >= 96).astype(jnp.int32)


def kernel(
    feat, gk, sqi, sqo, samp, read, fclip, keep, cot,
    llm, gout,
    sall, rall, srest, rrest, fta, ftb, cotb, wc, xs, cv, ac, sl, bm, gh, sqie, sqoe, pbuf, psl, psl2,
    p0, p1, obuf, prep, rsp, gap, rsg, gas, gad, acs, acd, gpf, acf, gpt, ges, ger, gos, gor, tks, tkr,
    cot_sem, sx_s, sx_r, sz_s, sz_r, sh_r, rz_s, rz_r, rx_s, rx_r, rh_r, ps_s, ps_r, pq_s, pq_r,
    e_sem, o_s, o_r, rp_s, rp_r, rg_s, rg_r, ga_s, ga_r, aa_s, aa_r, gp_s, gp_r, af_s, af_r,
    ge_sem, go_s, go_r, tk_sem,
):
    ctx = lax.axis_index("ctx")
    t = lax.axis_index("tp")
    k = lax.rem(ctx, 2)
    m = lax.div(ctx, 2)
    z = lax.rem(m, NZ)
    x = lax.div(m, NZ)
    chips = NX * NZ

    def dev(xx, zz, kk, tt):
        return ((xx * NZ + zz) * 2 + kk, tt)

    def chip(mm_, kk):
        return (lax.rem(mm_ + chips, chips) * 2 + kk, t)

    def zdev(d):
        return dev(x, lax.rem(z + d + NZ, NZ), k, t)

    def xdev(d):
        return dev(lax.rem(x + d + NX, NX), z, k, t)

    def tdev(d):
        return (ctx, lax.rem(t + d, NT))

    sibling = (m * 2 + (1 - k), t)
    t_low, t_high = lax.rem(t, 4), lax.div(t, 4)
    row_slot = 2 * z + t_high
    is_self = (t_low == x).astype(jnp.int32)

    def row_dev(i):
        return dev(t_low, i // 2, k, (i % 2) * 4 + x)

    def remote(src, dst, send, recv, where):
        return pltpu.make_async_remote_copy(
            src_ref=src, dst_ref=dst, send_sem=send, recv_sem=recv, device_id=where, device_id_type=MESH
        )

    sent = []

    def start(copy):
        copy.start()
        sent.append(copy)

    barrier = pltpu.get_barrier_semaphore()

    def hello(where):
        pl.semaphore_signal(barrier, inc=1, device_id=where, device_id_type=MESH)

    hello(sibling)
    for d in range(1, NX):
        hello(xdev(d))
    for d in range(1, NZ):
        hello(zdev(d))
    for d in range(1, NT):
        hello(tdev(d))
    hello(chip(m - 1, 1))

    @pl.when(k == 1)
    def _():
        hello(chip(m + 1, 0))
        hello(chip(m + 1, 1))

    for i in range(16):
        @pl.when(jnp.logical_not(jnp.logical_and(is_self == 1, row_slot == i)))
        def _(i=i):
            hello(row_dev(i))

    ftb[0:144, :] = jnp.zeros((144, 128), F32)
    fta[0:144, :] = samp[:, 0:128].astype(F32)
    ftb[0:144, 0:16] = samp[:, 128:144].astype(F32)
    rest = jnp.zeros((16, 128), F32)
    for s in range(8):
        sall[z, x, :, SLOT[s] : SLOT[s] + 128] = fta[pl.ds(s, 16, stride=8), :].astype(BF)
        tail = ftb[pl.ds(s, 16, stride=8), :]
        rest = rest + (tail if s == 0 else pltpu.roll(tail, 16 * s, 1))
    sall[z, x, :, 512:640] = rest.astype(BF)
    sall[z, x, :, 1152:1280] = fta[128:144, :].astype(BF)
    sall[z, x, :, 1280:1408] = ftb[128:144, :].astype(BF)
    rall[z, x, :, 0:1024] = read[0:16, :]
    last = read[16:18, :].astype(F32)
    for j in range(2):
        for p in range(8):
            fta[256 + j * 8 + p : 257 + j * 8 + p, :] = last[j : j + 1, 128 * p : 128 * p + 128]
    rall[z, x, :, 1024:1152] = fta[256:272, :].astype(BF)

    pl.semaphore_wait(barrier, 1 + (NX - 1) + (NZ - 1) + (NT - 1) + (1 + 2 * k) + 16 - is_self)

    for d in range(1, NX):
        start(remote(sall.at[z, x], sall.at[z, x], sx_s.at[d], sx_r.at[x], xdev(d)))
    for d in range(1, NZ):
        start(remote(rall.at[z, x], rall.at[z, x], rz_s.at[d], rz_r.at[z], zdev(d)))
    start(remote(cot, cotb.at[k], cot_sem.at[0], cot_sem.at[1], sibling))
    cotb[k] = cot[...]

    def wait_sx():
        for d in range(1, NX):
            o = lax.rem(x + d, NX)
            remote(sall.at[z, o], sall.at[z, o], sx_s.at[d], sx_r.at[o], xdev(d)).wait_recv()

    def zi(d):
        return lax.rem(z + d + 2 * NZ, NZ)

    def ring_s(i):
        up, down = zi(1 - i), zi(i - 1)
        if i < 4:
            start(remote(sall.at[up], sall.at[up], sz_s.at[i], sz_r.at[up], zdev(1)))
            start(remote(sall.at[down], sall.at[down], sz_s.at[i + 4], sz_r.at[down], zdev(-1)))
        else:
            start(remote(sall.at[up, 0:2], sall.at[up, 0:2], sz_s.at[4], sh_r.at[0], zdev(1)))
            start(remote(sall.at[down, 2:4], sall.at[down, 2:4], sz_s.at[8], sh_r.at[1], zdev(-1)))

    def wait_ring_s(i):
        up, down = zi(-i), zi(i)
        if i < 4:
            remote(sall.at[up], sall.at[up], sz_s.at[i], sz_r.at[up], zdev(1)).wait_recv()
            remote(sall.at[down], sall.at[down], sz_s.at[i + 4], sz_r.at[down], zdev(-1)).wait_recv()
        else:
            remote(sall.at[up, 0:2], sall.at[up, 0:2], sz_s.at[4], sh_r.at[0], zdev(1)).wait_recv()
            remote(sall.at[down, 2:4], sall.at[down, 2:4], sz_s.at[8], sh_r.at[1], zdev(-1)).wait_recv()

    def wait_rz():
        for d in range(1, NZ):
            o = zi(d)
            remote(rall.at[o, x], rall.at[o, x], rz_s.at[d], rz_r.at[o], zdev(d)).wait_recv()

    def xi(d):
        return lax.rem(x + d + NX, NX)

    def r_x(i):
        if i == 1:
            start(remote(rall.at[:, x], rall.at[:, x], rx_s.at[0], rx_r.at[0], xdev(1)))
            start(remote(rall.at[:, x], rall.at[:, x], rx_s.at[1], rx_r.at[1], xdev(-1)))
        else:
            up, down = xi(-1), xi(1)
            start(remote(rall.at[0:4, up], rall.at[0:4, up], rx_s.at[2], rh_r.at[0], xdev(1)))
            start(remote(rall.at[4:8, down], rall.at[4:8, down], rx_s.at[3], rh_r.at[1], xdev(-1)))

    def wait_r_x(i):
        if i == 1:
            up, down = xi(-1), xi(1)
            remote(rall.at[:, up], rall.at[:, up], rx_s.at[0], rx_r.at[0], xdev(1)).wait_recv()
            remote(rall.at[:, down], rall.at[:, down], rx_s.at[1], rx_r.at[1], xdev(-1)).wait_recv()
        else:
            far = xi(2)
            remote(rall.at[0:4, far], rall.at[0:4, far], rx_s.at[2], rh_r.at[0], xdev(1)).wait_recv()
            remote(rall.at[4:8, far], rall.at[4:8, far], rx_s.at[3], rh_r.at[1], xdev(-1)).wait_recv()

    widen = select(jnp.logical_and(iota((144, 256), 0) == iota((144, 256), 1), iota((144, 256), 1) < 144))
    cell = iota((256, 256), 0)
    cy, cx = cell >> 4, cell & 15
    inside = jnp.logical_and(
        jnp.logical_and(cy >= 1, cy <= 14), jnp.logical_and(cx >= 1, cx <= 14)
    )
    bm[...] = jnp.where(inside, 1.0, 0.0)
    into = select(padded_place(iota((256, 196), 1)) == iota((256, 196), 0))
    column = iota((48, 256), 1)
    spread = select(jnp.logical_and(column - 48 * third(column) == iota((48, 256), 0), column < 144))
    same_group = third(iota((144, 256), 0)) == third(iota((144, 256), 1))

    def centre(f):
        wide = mm(feat[f], widen).astype(BF)
        return mm(into, wide)

    def put_shifts(f, value):
        xs[f, 0, 16:272, :] = pltpu.roll(value, 1, 0).astype(BF)
        xs[f, 1, 16:272, :] = value.astype(BF)
        xs[f, 2, 16:272, :] = pltpu.roll(value, 255, 0).astype(BF)

    for f in range(2):
        for j in range(3):
            xs[f, j, 0:16, :] = jnp.zeros((16, 256), BF)
            xs[f, j, 272:288, :] = jnp.zeros((16, 256), BF)
        put_shifts(f, centre(f))
    for tap in range(9):
        dense = jnp.where(same_group, mm(gk[tap], spread), 0.0)
        wc[tap, 0:144, :] = dense.astype(BF)
        wc[tap, 144:256, :] = jnp.zeros((112, 256), BF)
    sqoe[...] = mm(sqo[...], widen).astype(BF)
    sqie[0:144, :] = sqi[...]
    sqie[144:256, :] = jnp.zeros((112, 288), BF)
    pbuf[...] = jnp.zeros((8, 256), F32)

    wait_sx()
    ring_s(1)

    def conv(f):
        total = jnp.zeros((256, 256), F32)
        for dy in range(3):
            for dx in range(3):
                total = total + mm(xs[f, dx, 16 * dy : 16 * dy + 256, :], wc[3 * dy + dx])
        cv[f] = total
        act = total * sigmoid(total) * bm[...]
        ac[f] = act
        pbuf[f : f + 1, :] = jnp.sum(act, axis=0, keepdims=True) * (1.0 / 196.0)

    conv(0)
    conv(1)
    psl[t] = exact(mm, pbuf[...], sqie[...])
    for d in range(1, NT):
        start(remote(psl.at[t], psl.at[t], ps_s.at[d], ps_r.at[t], tdev(d)))

    wait_rz()
    r_x(1)

    clips = fclip[...].astype(F32)
    lane = iota((64, 128), 1)
    row = iota((64, 128), 0)
    clip_col = jnp.sum(jnp.where(lane == 2 * row, clips, 0.0), axis=1, keepdims=True)
    before = jnp.logical_and((lane & 1) == 0, clips < clip_col)
    first = jnp.sum(jnp.where(before, 1.0, 0.0), axis=1, keepdims=True)
    lane16 = iota((64, 16), 1).astype(F32)
    kept = jnp.sum(jnp.where(lane16 == clip_col, keep[...].astype(F32), 0.0), axis=1, keepdims=True)
    place = (iota((64, 1), 0).astype(F32) - first) * 64.0

    def live(d):
        return jnp.where(place + jnp.asarray(d, jnp.int32).astype(F32) < kept, 1.0, 0.0)

    lane1 = iota((1, 128), 1)

    def pair_mask(c):
        now = jnp.sum(jnp.where(lane1 == 2 * c, clips, 0.0), axis=1, keepdims=True)
        was = jnp.sum(jnp.where(lane1 == 2 * c - 1, clips, 0.0), axis=1, keepdims=True)
        return jnp.where(jnp.logical_and(now == was, iota((1, 1), 0) + c > 0), 1.0, 0.0)

    mask0, mask1 = pair_mask(2 * m), pair_mask(2 * m + 1)

    for f in range(2):
        sl[f] = slope(cv[f]) * bm[...]

    def wait_slots(slots, send, recv):
        for d in range(1, NT):
            o = lax.rem(t + d, NT)
            remote(slots.at[o], slots.at[o], send.at[d], recv.at[o], tdev(d)).wait_recv()

    wait_slots(psl, ps_s, ps_r)
    squeezed = jnp.sum(psl[...], axis=0)
    excite = sigmoid(exact(mm, squeezed * sigmoid(squeezed), sqoe[...]))
    gather = select(patch_place(iota((256, 256), 0)) == iota((256, 256), 1))
    for f in range(2):
        hidden = xs[f, 1, 16:272, :].astype(F32) + ac[f] * excite[f : f + 1, :]
        taps = mm(gather, hidden.astype(BF))
        base = 4 * (1 - f)
        rest = jnp.zeros((64, 128), F32)
        for s in range(4):
            tail = taps[64 * s : 64 * s + 64, 128:256]
            by = 16 * (s + base)
            rest = rest + (tail if by == 0 else pltpu.roll(tail, by, 1))
        main = taps[:, 0:128].astype(BF)
        if f == 0:
            mine = pl.ds(pl.multiple_of(64 * k, 64), 64)
            p1[mine, 0:128] = rest.astype(BF)
            for s in range(4):
                p1[mine, 128 * (s + 1) : 128 * (s + 2)] = main[64 * s : 64 * s + 64]
            start(remote(p1.at[mine], p1.at[mine], e_sem.at[0], e_sem.at[1], sibling))
        else:
            obuf[:, 512:640] = rest.astype(BF)
            for s in range(4):
                obuf[:, 128 * s : 128 * (s + 1)] = main[64 * s : 64 * s + 64]

    @pl.when(k == 0)
    def _():
        p0[64:128, :] = obuf[...]
        remote(obuf, p0.at[64:128], o_s.at[0], o_r.at[1], sibling).start()

    @pl.when(k == 1)
    def _():
        remote(obuf, p0.at[0:64], o_s.at[0], o_r.at[0], chip(m + 1, 1)).start()
        remote(obuf, p0.at[0:64], o_s.at[1], o_r.at[0], chip(m + 1, 0)).start()

    wait_ring_s(1)
    ring_s(2)
    wait_r_x(1)
    r_x(2)
    wait_ring_s(2)
    ring_s(3)

    other = pl.ds(pl.multiple_of(64 * (1 - k), 64), 64)
    wait_r_x(2)
    fta[...] = rall[:, :, :, 1024:1152].reshape(512, 128).astype(F32)
    for p in range(8):
        rrest[0:64, 128 * p : 128 * p + 128] = fta[pl.ds(p, 64, stride=8), :].astype(BF)
    rrest[64:128, :] = jnp.zeros((64, 1024), BF)
    remote(cot, cotb.at[1 - k], cot_sem.at[0], cot_sem.at[1], sibling).wait_recv()
    back = cotb[...].reshape(128, 1024)
    alive = jnp.concatenate([live(2 * m), live(2 * m + 1)], axis=0)
    gap[:, :, 0:512] = (
        (mmt(back, rall[:, :, :, 0:1024].reshape(512, 1024)) * alive).astype(BF).reshape(8, 16, 512)
    )
    gap[:, :, 512:640] = (mmt(back, rrest[...]) * alive).astype(BF).reshape(8, 16, 128)

    def scatter(parts, slots, send, recv):
        for d in range(1, NT):
            o = lax.rem(t + d, NT)
            start(remote(parts.at[o], slots.at[t], send.at[d], recv.at[t], tdev(d)))

    def scattered(parts, slots, send, recv):
        wait_slots(slots, send, recv)
        total = parts[t].astype(F32)
        for d in range(1, NT):
            total = total + slots[lax.rem(t + d, NT)].astype(F32)
        return total

    scatter(gap, rsg, rg_s, rg_r)

    wait_ring_s(3)
    ring_s(4)

    remote(p1.at[other], p1.at[other], e_sem.at[0], e_sem.at[1], sibling).wait_recv()
    remote(obuf, p0.at[0:64], o_s.at[0], o_r.at[0], sibling).wait_recv()

    @pl.when(k == 1)
    def _():
        remote(obuf, p0.at[64:128], o_s.at[0], o_r.at[1], sibling).wait_recv()

    wait_ring_s(4)
    fta[...] = sall[:, :, :, 1152:1280].reshape(512, 128).astype(F32)
    ftb[...] = sall[:, :, :, 1280:1408].reshape(512, 128).astype(F32)
    rest = jnp.zeros((64, 128), F32)
    for s in range(8):
        srest[0:64, SLOT[s] : SLOT[s] + 128] = fta[pl.ds(s, 64, stride=8), :].astype(BF)
        tail = ftb[pl.ds(s, 64, stride=8), :]
        rest = rest + (tail if s == 0 else pltpu.roll(tail, 16 * s, 1))
    srest[0:64, 512:640] = rest.astype(BF)
    srest[64:128, :] = jnp.zeros((64, 1152), BF)

    mask_col = jnp.concatenate(
        [jnp.broadcast_to(mask0, (64, 1)), jnp.broadcast_to(mask1, (64, 1))], axis=0
    )

    def pre_part(w0, w1):
        return mmt(p0[...], w0) * mask_col + mmt(p1[...], w1)

    prep[:, :, 0:512] = (
        pre_part(sall[:, :, :, 0:640].reshape(512, 640), sall[:, :, :, 512:1152].reshape(512, 640))
        .astype(BF)
        .reshape(8, 16, 512)
    )
    prep[:, :, 512:640] = pre_part(srest[:, 0:640], srest[:, 512:1152]).astype(BF).reshape(8, 16, 128)
    scatter(prep, rsp, rp_s, rp_r)

    def put_rows(src, value, dst, send, recv):
        for i in range(16):
            src[i] = value[i : i + 1, :]
        for i in range(16):
            own = jnp.logical_and(is_self == 1, row_slot == i)

            @pl.when(own)
            def _(i=i):
                dst[i] = src[i]

            @pl.when(jnp.logical_not(own))
            def _(i=i):
                remote(src.at[i], dst.at[row_slot], send.at[i], recv.at[row_slot], row_dev(i)).start()

    def get_rows(src, dst, send, recv):
        for i in range(16):
            own = jnp.logical_and(is_self == 1, row_slot == i)

            @pl.when(jnp.logical_not(own))
            def _(i=i):
                remote(src.at[i], dst.at[i], send.at[i], recv.at[i], row_dev(i)).wait()

        return jnp.concatenate([dst[i] for i in range(16)], axis=0)

    put_rows(gas, scattered(gap, rsg, rg_s, rg_r), gad, ga_s, ga_r)
    pre = scattered(prep, rsp, rp_s, rp_r)
    put_rows(acs, (pre * sigmoid(pre)).astype(BF).astype(F32), acd, aa_s, aa_r)
    pre_slope = slope(pre)

    gpf[t] = (get_rows(gas, gad, ga_s, ga_r) * pre_slope).astype(BF)
    for d in range(1, NT):
        start(remote(gpf.at[t], gpf.at[t], gp_s.at[d], gp_r.at[t], tdev(d)))
    acf[t] = get_rows(acs, acd, aa_s, aa_r).astype(BF)
    for d in range(1, NT):
        start(remote(acf.at[t], acf.at[t], af_s.at[d], af_r.at[t], tdev(d)))

    wait_slots(gpf, gp_s, gp_r)
    grads = gpf[...].reshape(128, 640)
    gpt[...] = mm(grads[:, 0:512], sall[:, :, :, 0:1152].reshape(512, 1152)) + mm(grads[:, 512:640], srest[...])
    ges[...] = gpt[other, 512:1152].astype(BF)
    start(remote(ges, ger, ge_sem.at[0], ge_sem.at[1], sibling))
    gos[0] = (gpt[0:64, 0:640] * mask0).astype(BF)
    gos[1] = (gpt[64:128, 0:640] * mask1).astype(BF)
    start(remote(gos.at[0], gor.at[k], go_s.at[0], go_r.at[k], chip(m - 1, 1)))

    @pl.when(k == 1)
    def _():
        remote(gos.at[1], gor.at[1], go_s.at[1], go_r.at[1], sibling).start()

    @pl.when(k == 0)
    def _():
        gor[0] = gos[1]

    wait_slots(acf, af_s, af_r)
    acts = acf[...].reshape(128, 640)
    part = mm(acts[:, 0:512], rall[:, :, :, 0:1024].reshape(512, 1024)) + mm(acts[:, 512:640], rrest[...])
    low, high = part[0:64], part[64:128]
    kf = k.astype(F32)
    tks[...] = (low * kf + high * (1.0 - kf)).astype(BF)
    start(remote(tks, tkr, tk_sem.at[0], tk_sem.at[1], sibling))
    own_tokens = low * (1.0 - kf) + high * kf

    remote(ges, ger, ge_sem.at[0], ge_sem.at[1], sibling).wait_recv()
    remote(gos.at[0], gor.at[1], go_s.at[0], go_r.at[1], sibling).wait_recv()

    @pl.when(k == 1)
    def _():
        remote(gos.at[0], gor.at[0], go_s.at[0], go_r.at[0], sibling).wait_recv()

    mine = pl.ds(pl.multiple_of(64 * k, 64), 64)
    even = gpt[mine, 512:1152] + ger[...].astype(F32)
    odd = gor[0].astype(F32) + gor[1].astype(F32)
    ungather = select(patch_place(iota((256, 256), 1)) == iota((256, 256), 0))
    narrow = iota((64, 128), 1) < 16
    for f in range(2):
        if f == 0:
            tile, mains, base = even[:, 0:128], even[:, 128:640], 4
        else:
            tile, mains, base = odd[:, 512:640], odd[:, 0:512], 0
        main = jnp.concatenate([mains[:, 128 * s : 128 * s + 128] for s in range(4)], axis=0)
        tails = []
        for s in range(4):
            by = (128 - 16 * (s + base)) % 128
            tails.append(jnp.where(narrow, tile if by == 0 else pltpu.roll(tile, by, 1), 0.0))
        taps = jnp.concatenate([main, jnp.concatenate(tails, axis=0)], axis=1)
        top = taps.astype(BF)
        bottom = (taps - top.astype(F32)).astype(BF)
        grad = (mm(ungather, top) + mm(ungather, bottom)) * bm[...]
        gh[f] = grad
        pbuf[f : f + 1, :] = jnp.sum(grad * ac[f], axis=0, keepdims=True)

    inner = pbuf[...] * excite * (1.0 - excite)
    psl2[t] = exact(mmt, inner, sqoe[...])
    for d in range(1, NT):
        start(remote(psl2.at[t], psl2.at[t], pq_s.at[d], pq_r.at[t], tdev(d)))

    remote(tks, tkr, tk_sem.at[0], tk_sem.at[1], sibling).wait_recv()
    llm[...] = ((own_tokens + tkr[...].astype(F32)) * live(ctx)).astype(BF)

    wait_slots(psl2, pq_s, pq_r)
    grad_squeezed = jnp.sum(psl2[...], axis=0) * slope(squeezed)
    grad_pooled = exact(mmt, grad_squeezed, sqie[...]) * (1.0 / 196.0)
    outof = select(padded_place(iota((196, 256), 0)) == iota((196, 256), 1))
    for f in range(2):
        grad_active = gh[f] * excite[f : f + 1, :] + grad_pooled[f : f + 1, :]
        put_shifts(f, grad_active * sl[f])
        total = gh[f]
        for dy in range(3):
            for dx in range(3):
                total = total + mmt(xs[f, 2 - dx, 16 * (2 - dy) : 16 * (2 - dy) + 256, :], wc[3 * dy + dx])
        gout[f] = mm(outof, total.astype(BF))[:, 0:144].astype(BF)

    for copy in sent:
        copy.wait_send()
    remote(obuf, p0.at[0:64], o_s.at[0], o_r.at[0], sibling).wait_send()

    @pl.when(k == 1)
    def _():
        remote(obuf, p0.at[0:64], o_s.at[1], o_r.at[0], sibling).wait_send()
        remote(gos.at[1], gor.at[1], go_s.at[1], go_r.at[1], sibling).wait_send()


def per_device(features, group_kernel, squeeze_in, squeeze_out, sampler_kernel, readout_kernel, frame_clip, clip_keep, token_cotangent):
    V = pltpu.VMEM
    dma = pltpu.SemaphoreType.DMA
    scratch = [
        V((NZ, NX, 16, 1408), BF),
        V((NZ, NX, 16, 1152), BF),
        V((128, 1152), BF),
        V((128, 1024), BF),
        V((512, 128), F32),
        V((512, 128), F32),
        V((2, 64, 1024), BF),
        V((9, 256, 256), BF),
        V((2, 3, 288, 256), BF),
        V((2, 256, 256), F32),
        V((2, 256, 256), F32),
        V((2, 256, 256), F32),
        V((256, 256), F32),
        V((2, 256, 256), F32),
        V((256, 288), BF),
        V((288, 256), BF),
        V((8, 256), F32),
        V((NT, 8, 288), F32),
        V((NT, 8, 288), F32),
        V((128, 640), BF),
        V((128, 640), BF),
        V((64, 640), BF),
        V((8, 16, 640), BF),
        V((8, 16, 640), BF),
        V((8, 16, 640), BF),
        V((8, 16, 640), BF),
        V((16, 1, 640), F32),
        V((16, 1, 640), F32),
        V((16, 1, 640), F32),
        V((16, 1, 640), F32),
        V((8, 16, 640), BF),
        V((8, 16, 640), BF),
        V((128, 1152), F32),
        V((64, 640), BF),
        V((64, 640), BF),
        V((2, 64, 640), BF),
        V((2, 64, 640), BF),
        V((64, 1024), BF),
        V((64, 1024), BF),
        dma((2,)),
        dma((4,)), dma((4,)),
        dma((9,)), dma((8,)), dma((2,)),
        dma((8,)), dma((8,)),
        dma((4,)), dma((2,)), dma((2,)),
        dma((8,)), dma((8,)),
        dma((8,)), dma((8,)),
        dma((2,)),
        dma((2,)), dma((2,)),
        dma((8,)), dma((8,)),
        dma((8,)), dma((8,)),
        dma((16,)), dma((16,)),
        dma((16,)), dma((16,)),
        dma((8,)), dma((8,)),
        dma((8,)), dma((8,)),
        dma((2,)),
        dma((2,)), dma((2,)),
        dma((2,)),
    ]
    spec = pl.BlockSpec(memory_space=pltpu.VMEM)
    return pl.pallas_call(
        kernel,
        out_shape=(jax.ShapeDtypeStruct((64, 1024), BF), jax.ShapeDtypeStruct((2, 196, 144), BF)),
        in_specs=[spec] * 9,
        out_specs=(spec, spec),
        scratch_shapes=scratch,
        compiler_params=pltpu.CompilerParams(
            collective_id=0, has_side_effects=True, vmem_limit_bytes=48 * 1024 * 1024
        ),
        cost_estimate=pl.CostEstimate(flops=3_000_000_000, bytes_accessed=1_000_000, transcendentals=1_000_000),
        name="connector",
    )(
        features,
        group_kernel,
        squeeze_in,
        squeeze_out,
        sampler_kernel.reshape(144, 144),
        readout_kernel,
        frame_clip.reshape(1, 128),
        clip_keep.reshape(1, 16),
        token_cotangent,
    )


def solution(mesh):
    placed = (
        P("ctx", None, "tp"),
        P(None, "tp", None),
        P("tp", None),
        P(None, "tp"),
        P("ctx", None, "tp"),
        P("ctx", "tp"),
        P(),
        P(),
        P("ctx", "tp"),
    )
    return jax.shard_map(
        per_device,
        mesh=mesh,
        in_specs=placed,
        out_specs=(P("ctx", "tp"), P("ctx", None, "tp")),
        check_vma=False,
    )
```

time: 349 us -> 81.8 us (0.23)
  the two profiles are of different devices: /device:TPU:1 before, /device:TPU:4 now
where the time goes in v1:
time: 81.8 us; the launch traced here: 81.7 us
  Pallas kernels  76.5 us (94%)
  local copies, waits for them, and re-layouts  4.41 us (5%)
    pallas_call x1, Pallas kernels, per_device(): pl.pallas_call(kernel, out_shape=(jax.ShapeDtypeStruct((64, 1024), BF), j...  76.5 us
    unnamed x20, local copies, waits for them, and re-layouts  3.61 us

profile of v1, /device:TPU:4, one launch (start us, length us, event | category | flops | bytes accessed | tf_op | source)
XLA Modules:
  0.0 81.7 jit_solution(17017948326692820071)
XLA Ops:
  0.6 0.0 copy-start.7
  0.6 1.0 %copy.13.sqo = bf16[288,144]{1,0:T(8,128)(2,1)S(1)} copy(bf16[288,144]{0,1:T(8,128)(2,1)} %param.12) | data formatting | bytes 165888 | tf_op args[3]
  1.7 0.0 copy-done.7
  1.7 0.0 copy-start.6
  1.7 0.1 copy.11.feat
  1.8 0.8 copy-done.6
  2.6 0.0 copy-start
  2.6 0.0 copy-start.1
  2.6 0.0 copy-start.2
  2.6 0.0 copy-start.3
  2.6 0.0 copy-start.4
  2.7 0.0 copy-start.5
  2.7 0.3 copy.12.gk
  2.9 0.6 copy-done
  3.5 0.1 copy-done.1
  3.6 0.0 copy-done.2
  3.6 0.0 copy-done.3
  3.6 0.0 copy-done.4
  3.6 0.0 copy-done.5
  3.6 76.5 %connector.1 = (bf16[64,1024]{1,0:T(8,128)(2,1)S(1)}, bf16[2,196,144]{2,1,0:T(8,128)(2,1)S(1)}) custom-call(bf16[2,196,144]{2,1,0:T(8,128)(2,1)S(1)} %copy.11.feat, bf16[9,144,48]{2,1,0:T(8,128)(2,1)S(1)} %copy.12.gk, bf16[144,288]{1,0:T(8,128)(2,1)S(1)} %copy-done.1, bf16[288,144]{1,0:T(8,128)(2,1)S(1)} %copy.13.sqo, bf16[144,144]{1,0:T(8,128)(2,1)S(1)} %bitcast.3, ...), custom_call_target="tpu_custom_call" | custom-call | flops 3000000000 | bytes 1000000 | tf_op jit(solution)/shard_map/connector/pallas_call | solution.py:597
  80.2 0.8 copy.14
  81.0 0.7 copy.16
Async XLA Ops:
  0.6 1.1 %copy-start.7 = (bf16[2,196,144]{1,2,0:T(8,128)(2,1)S(1)}, bf16[2,196,144]{1,2,0:T(8,128)(2,1)}, u32[]{:S(2)}) copy-start(bf16[2,196,144]{1,2,0:T(8,128)(2,1)} %param.9) | copy-start | bytes 338692
  1.7 0.9 %copy-start.6 = (bf16[9,144,48]{1,2,0:T(8,128)(2,1)S(1)}, bf16[9,144,48]{1,2,0:T(8,128)(2,1)}, u32[]{:S(2)}) copy-start(bf16[9,144,48]{1,2,0:T(8,128)(2,1)} %param.10) | copy-start | bytes 373252
  2.6 0.9 %copy-start = (bf16[64,1024]{1,0:T(8,128)(2,1)S(1)}, bf16[64,1024]{1,0:T(8,128)(2,1)}, u32[]{:S(2)}) copy-start(bf16[64,1024]{1,0:T(8,128)(2,1)} %cot.1) | copy-start | bytes 393220
  2.6 1.0 %copy-start.1 = (bf16[144,288]{1,0:T(8,128)(2,1)S(1)}, bf16[144,288]{1,0:T(8,128)(2,1)}, u32[]{:S(2)}) copy-start(bf16[144,288]{1,0:T(8,128)(2,1)} %sqi.1) | copy-start | bytes 248836
  2.6 1.0 %copy-start.2 = (bf16[18,8,144]{2,1,0:T(8,128)(2,1)S(1)}, bf16[18,8,144]{2,1,0:T(8,128)(2,1)}, u32[]{:S(2)}) copy-start(bf16[18,8,144]{2,1,0:T(8,128)(2,1)} %param.13) | copy-start | bytes 124420
  2.6 1.0 %copy-start.3 = (bf16[18,1024]{1,0:T(8,128)(2,1)S(1)}, bf16[18,1024]{1,0:T(8,128)(2,1)}, u32[]{:S(2)}) copy-start(bf16[18,1024]{1,0:T(8,128)(2,1)} %read.1) | copy-start | bytes 110596
  2.6 1.0 %copy-start.4 = (s32[128]{0:T(128)S(1)}, s32[128]{0:T(128)}, u32[]{:S(2)}) copy-start(s32[128]{0:T(128)} %param.15) | copy-start | bytes 1540
  2.7 1.0 %copy-start.5 = (s32[16]{0:T(128)S(1)}, s32[16]{0:T(128)}, u32[]{:S(2)}) copy-start(s32[16]{0:T(128)} %param.16) | copy-start | bytes 196

commit v2 on v1

v2 whole, which is shorter than its diff:
```python
import jax
import jax.numpy as jnp
from jax import lax
from jax.experimental import pallas as pl
from jax.experimental.pallas import tpu as pltpu
from jax.sharding import PartitionSpec as P

NX, NZ, NT = 4, 8, 8
BF = jnp.bfloat16
F32 = jnp.float32
MESH = pl.DeviceIdType.MESH
SLOT = (0, 128, 256, 384, 640, 768, 896, 1024)


def iota(shape, dim):
    return lax.broadcasted_iota(jnp.int32, shape, dim)


def select(hit):
    return jnp.where(hit, 1.0, 0.0).astype(BF)


def mm(a, b):
    return jnp.dot(a, b, preferred_element_type=F32)


def mmt(a, b):
    return lax.dot_general(a, b, (((1,), (1,)), ((), ())), preferred_element_type=F32)


def exact(dot, value, weight):
    high = value.astype(BF)
    left = value - high.astype(F32)
    middle = left.astype(BF)
    low = (left - middle.astype(F32)).astype(BF)
    return dot(high, weight) + (dot(middle, weight) + dot(low, weight))


def sigmoid(v):
    return jax.nn.sigmoid(v)


def slope(v):
    s = sigmoid(v)
    return s * (1.0 + v * (1.0 - s))


def padded_place(cell):
    row = (cell * 4682) >> 16
    return (row + 1) * 16 + (cell - 14 * row) + 1


def token_at(row):
    return 4 * (row & 15) + 2 * ((row >> 4) & 1) + ((row >> 5) & 1)


def patch_place(r):
    s = r >> 6
    token = token_at(r & 63)
    a = token >> 3
    b = token & 7
    return (2 * a + (s >> 1)) * 16 + 2 * b + (s & 1)


def third(v):
    return (v >= 48).astype(jnp.int32) + (v >= 96).astype(jnp.int32)


def kernel(
    feat_h, gk_h, sqi_h, sqo_h, samp_h, read_h, fclip, keep, cot_h,
    llm, gout,
    feat, gk, samp, read,
    sall, rall, srest, rrest, fta, ftb, cotb, wc, xs, cv, ac, sl, bm, gh, sqie, sqoe, pbuf, psl, psl2,
    p0, p1, obuf, prep, rsp, gap, rsg, gas, gad, acs, acd, gpf, acf, gpt, ges, ger, gos, gor, tks, tkr,
    load, cot_sem, s_out, s_in, r_out, r_in, pair, e_sem, o_s, o_r, ge_sem, go_s, go_r, tk_sem,
):
    ctx = lax.axis_index("ctx")
    t = lax.axis_index("tp")
    k = lax.rem(ctx, 2)
    m = lax.div(ctx, 2)
    z = lax.rem(m, NZ)
    x = lax.div(m, NZ)
    chips = NX * NZ

    def dev(xx, zz, kk, tt):
        return ((xx * NZ + zz) * 2 + kk, tt)

    def chip(mm_, kk):
        return (lax.rem(mm_ + chips, chips) * 2 + kk, t)

    def zdev(d):
        return dev(x, lax.rem(z + d + NZ, NZ), k, t)

    def xdev(d):
        return dev(lax.rem(x + d + NX, NX), z, k, t)

    def tdev(d):
        return (ctx, lax.rem(t + d, NT))

    sibling = (m * 2 + (1 - k), t)
    twist = lax.rem(m + lax.div(t, 4), 2)
    row_slot = lax.div(m, 2)
    is_self = (t < 4).astype(jnp.int32)

    def frame_chunk(o):
        return 4 * lax.rem(o, 2) + 2 * lax.rem(lax.div(o, 2), 2) + lax.rem(lax.div(o, 4) + m, 2)

    def decoder_chunk(o):
        return 4 * lax.rem(lax.div(o, 2), 2) + 2 * lax.rem(o, 2) + lax.rem(lax.div(o, 4) + m, 2)

    def row_dev(i):
        return ((2 * i + twist) * 2 + k, t)

    def remote(src, dst, send, recv, where):
        return pltpu.make_async_remote_copy(
            src_ref=src, dst_ref=dst, send_sem=send, recv_sem=recv, device_id=where, device_id_type=MESH
        )

    def exchange(source, slots, slot, which):
        for d in range(1, NT):
            o = lax.rem(t + d, NT)
            remote(source(o), slots.at[slot], pair.at[which, 0], pair.at[which, 1], tdev(d)).start()
        all_of = remote(slots.at[0 : NT - 1], slots.at[0 : NT - 1], pair.at[which, 0], pair.at[which, 1], tdev(1))
        leaving.append(all_of.wait_send)
        return all_of.wait_recv

    leaving = []
    coming = {}

    def start(copy):
        copy.start()
        leaving.append(copy.wait_send)

    def arrive(*names):
        for name in names:
            coming.pop(name)()

    def finish():
        arrive(*list(coming))
        for left in leaving:
            left()

    barrier = pltpu.get_barrier_semaphore()

    def hello(where):
        pl.semaphore_signal(barrier, inc=1, device_id=where, device_id_type=MESH)

    local = []
    for i, (src, dst) in enumerate(
        (
            (read_h, read), (samp_h, samp), (feat_h, feat), (gk_h, gk), (cot_h, cotb.at[k]),
            (sqi_h, sqie.at[0:144]), (sqo_h, sqoe.at[0:144]),
        )
    ):
        local.append(pltpu.make_async_copy(src, dst, load.at[i]))
        local[-1].start()

    hello(sibling)
    for d in range(1, NX):
        hello(xdev(d))
    hello(zdev(1))
    hello(zdev(-1))
    for d in range(1, NT):
        hello(tdev(d))
    hello(chip(m - 1, 1))

    @pl.when(k == 1)
    def _():
        hello(chip(m + 1, 0))
        hello(chip(m + 1, 1))

    trade = [lax.rem(row_slot + j, 16) for j in range(16)]

    @pl.when(is_self == 0)
    def _():
        hello(row_dev(trade[0]))

    for j in range(1, 16):
        hello(row_dev(trade[j]))

    own = 4 * z + x
    local[0].wait()
    rall[own, :, 0:1024] = read[0:16, :]
    last = read[16:18, :].astype(F32)
    for j in range(2):
        for p in range(8):
            fta[256 + j * 8 + p : 257 + j * 8 + p, :] = last[j : j + 1, 128 * p : 128 * p + 128]
    rall[own, :, 1024:1152] = fta[256:272, :].astype(BF)
    local[1].wait()
    ftb[0:144, :] = jnp.zeros((144, 128), F32)
    fta[0:144, :] = samp[:, 0:128].astype(F32)
    ftb[0:144, 0:16] = samp[:, 128:144].astype(F32)
    rest = jnp.zeros((16, 128), F32)
    for s in range(8):
        sall[own, :, SLOT[s] : SLOT[s] + 128] = fta[pl.ds(s, 16, stride=8), :].astype(BF)
        tail = ftb[pl.ds(s, 16, stride=8), :]
        rest = rest + (tail if s == 0 else pltpu.roll(tail, 16 * s, 1))
    sall[own, :, 512:640] = rest.astype(BF)
    sall[own, :, 1152:1280] = fta[128:144, :].astype(BF)
    sall[own, :, 1280:1408] = ftb[128:144, :].astype(BF)

    pl.semaphore_wait(barrier, 1 + (NX - 1) + 2 + (NT - 1) + (1 + 2 * k) + 16 - is_self)

    def zi(d):
        return lax.rem(z + d + NZ, NZ)

    def xi(e):
        return lax.rem(x + e, NX)

    def hop(d):
        return {-1: 0, -2: 1, -3: 2, 1: 3, 2: 4, 3: 5, 4: 6}[d]

    class Gather:
        def __init__(self, ref, out, into, way):
            self.ref, self.out, self.into, self.way = ref, out, into, way

        def block(self, d, e):
            return self.ref.at[4 * zi(d) + xi(e)]

        def send(self, d, e, sem, where):
            remote(self.block(d, e), self.block(d, e), self.out.at[0], self.into.at[sem], where).start()

        def got(self, d, e, sem):
            remote(self.block(d, e), self.block(d, e), self.out.at[0], self.into.at[sem], sibling).wait_recv()

        def a_z(self, e):
            if e:
                self.got(0, e, e)
            self.send(0, e, 4 + 7 * e + hop(-1), zdev(1))
            self.send(0, e, 4 + 7 * e + hop(1), zdev(-1))

        def a_start(self):
            for e in (1, 3, 2):
                self.send(0, 0, (-e) % 4, xdev(e))
            self.a_z(0)

        def a_ring(self, i, *columns):
            for e in columns:
                at = 4 + 7 * e
                self.got(-i, e, at + hop(-i))
                self.got(i, e, at + hop(i))
                if i < 3:
                    self.send(-i, e, at + hop(-i - 1), zdev(1))
                    self.send(i, e, at + hop(i + 1), zdev(-1))
                else:
                    way = 1 if e % 2 == 0 else -1
                    self.send(-3 * way, e, at + hop(4), zdev(way))

        def a_end(self):
            for e in (0, 1, 3, 2):
                self.got(4, e, 4 + 7 * e + hop(4))

        def b_at(self, d, e):
            return 7 + 3 * (d % 8) + e - 1

        def b_x(self, d):
            self.send(d, 0, self.b_at(d, 3), xdev(1))
            self.send(d, 0, self.b_at(d, 1), xdev(-1))

        def b_start(self):
            self.send(0, 0, hop(-1), zdev(1))
            self.send(0, 0, hop(1), zdev(-1))
            self.b_x(0)

        def b_ring(self, i):
            if i == 4:
                self.got(4, 0, hop(4))
                self.b_x(4)
                return
            self.got(-i, 0, hop(-i))
            self.got(i, 0, hop(i))
            if i < 3:
                self.send(-i, 0, hop(-i - 1), zdev(1))
                self.send(i, 0, hop(i + 1), zdev(-1))
            else:
                self.send(-3 * self.way, 0, hop(4), zdev(self.way))
            self.b_x(-i)
            self.b_x(i)

        def b_pass(self, *rows):
            for d in rows:
                e = 3 if d % 2 == 0 else 1
                self.got(d, e, self.b_at(d, e))
                self.send(d, e, self.b_at(d, 2), xdev(1 if e == 3 else -1))

        def b_end(self):
            for d in (0, 1, -1, 2, -2, 3, -3, 4):
                e = 1 if d % 2 == 0 else 3
                self.got(d, e, self.b_at(d, e))
            for d in (0, 1, -1, 2, -2, 3, -3, 4):
                self.got(d, 2, self.b_at(d, 2))

        def end(self):
            cores(self.a_end, self.b_end)

    def cores(zero, one):
        pl.when(k == 0)(lambda: zero() and None)
        pl.when(k == 1)(lambda: one() and None)

    R = Gather(rall, r_out, r_in, 1)
    S = Gather(sall, s_out, s_in, -1)

    def weights_sent():
        remote(rall.at[0:31], rall.at[0:31], r_out.at[0], r_out.at[0], sibling).wait_send()
        remote(sall.at[0:31], sall.at[0:31], s_out.at[0], s_out.at[0], sibling).wait_send()

    leaving.append(weights_sent)

    def pump(n):
        cores(
            [
                lambda: (R.a_start(), S.a_start()),
                lambda: (R.a_z(1), R.a_z(3)),
                lambda: (R.a_z(2), R.a_ring(1, 0)),
                lambda: R.a_ring(1, 1, 3),
                lambda: (R.a_ring(1, 2), R.a_ring(2, 0), S.a_z(1), S.a_z(3)),
                lambda: R.a_ring(2, 1, 3),
                lambda: (R.a_ring(2, 2), R.a_ring(3, 0), S.a_z(2)),
                lambda: (R.a_ring(3, 1, 3, 2), S.a_ring(1, 0)),
                lambda: S.a_ring(1, 1, 3, 2),
                lambda: S.a_ring(2, 0, 1),
                lambda: S.a_ring(2, 3, 2),
                lambda: S.a_ring(3, 0, 1),
                lambda: S.a_ring(3, 3, 2),
            ][n],
            [
                lambda: (R.b_start(), S.b_start()),
                lambda: R.b_ring(1),
                lambda: (R.b_ring(2), R.b_pass(0)),
                lambda: (R.b_ring(3), S.b_ring(1)),
                lambda: (R.b_ring(4), R.b_pass(1, -1)),
                lambda: (R.b_pass(2, -2), S.b_ring(2)),
                lambda: (R.b_pass(3, -3, 4), S.b_ring(3), S.b_pass(0)),
                lambda: S.b_ring(4),
                lambda: S.b_pass(1, -1),
                lambda: S.b_pass(2, -2),
                lambda: S.b_pass(3, -3),
                lambda: S.b_pass(4),
                lambda: None,
            ][n],
        )

    pump(0)
    start(remote(cot_h, cotb.at[k], cot_sem.at[0], cot_sem.at[1], sibling))
    coming["cot"] = remote(cot_h, cotb.at[1 - k], cot_sem.at[0], cot_sem.at[1], sibling).wait_recv
    cell = iota((256, 256), 0)
    cy, cx = cell >> 4, cell & 15
    inside = jnp.logical_and(
        jnp.logical_and(cy >= 1, cy <= 14), jnp.logical_and(cx >= 1, cx <= 14)
    )
    bm[...] = jnp.where(inside, 1.0, 0.0)
    into = select(padded_place(iota((256, 196), 1)) == iota((256, 196), 0))
    channel = iota((144, 48), 0)
    spread = select(channel - 48 * third(channel) == iota((144, 48), 1))
    same_group = third(iota((144, 144), 0)) == third(iota((144, 144), 1))
    blank = jnp.zeros((112, 196), BF)

    def centre(f):
        if f == 0:
            local[2].wait()
        return mmt(into, jnp.concatenate([feat[f], blank], axis=0))

    def put_shifts(f, value):
        xs[0, f, 16:272, :] = pltpu.roll(value, 1, 0).astype(BF)
        xs[1, f, 16:272, :] = value.astype(BF)
        xs[2, f, 16:272, :] = pltpu.roll(value, 255, 0).astype(BF)

    for f in range(2):
        for j in range(3):
            xs[j, f, 0:16, :] = jnp.zeros((16, 256), BF)
            xs[j, f, 272:288, :] = jnp.zeros((16, 256), BF)
        put_shifts(f, centre(f))
        pump(1 + f)
    local[3].wait()
    for tap in range(9):
        wc[tap] = jnp.zeros((256, 256), BF)
        dense = jnp.where(same_group, mm(spread, gk[tap]), 0.0)
        wc[tap, 0:144, 0:144] = dense.astype(BF)
        if tap == 4:
            pump(3)
    sqoe[144:256, :] = jnp.zeros((112, 288), BF)
    sqie[144:256, :] = jnp.zeros((112, 288), BF)
    pbuf[...] = jnp.zeros((8, 256), F32)
    pump(4)

    both = jnp.zeros((512, 256), F32)
    for dy in range(3):
        for dx in range(3):
            window = xs[dx, :, 16 * dy : 16 * dy + 256, :].reshape(512, 256)
            both = both + mmt(window, wc[3 * dy + dx])
        pump(5 + dy)
    for f in range(2):
        total = both[256 * f : 256 * f + 256]
        cv[f] = total
        act = total * sigmoid(total) * bm[...]
        ac[f] = act
        pbuf[f : f + 1, :] = jnp.sum(act, axis=0, keepdims=True) * (1.0 / 196.0)
    local[5].wait()
    local[6].wait()

    def put_sums(slots, sums, which):
        slots[t] = jnp.zeros((1, 768), F32)
        slots[t, :, 0:288] = sums[0:1]
        slots[t, :, 384:672] = sums[1:2]
        return exchange(lambda o: slots.at[t], slots, t, which)

    def get_sums(slots):
        both_rows = jnp.sum(slots[...], axis=0)
        return jnp.concatenate([both_rows[:, 0:288], both_rows[:, 384:672], jnp.zeros((6, 288), F32)], axis=0)

    coming["ps"] = put_sums(psl, exact(mm, pbuf[...], sqie[...]), 0)
    pump(8)

    clips = fclip[...].astype(F32)
    lane = iota((64, 128), 1)
    clip_col = jnp.sum(jnp.where(lane == 2 * token_at(iota((64, 128), 0)), clips, 0.0), axis=1, keepdims=True)
    before = jnp.logical_and((lane & 1) == 0, clips < clip_col)
    first = jnp.sum(jnp.where(before, 1.0, 0.0), axis=1, keepdims=True)
    lane16 = iota((64, 16), 1).astype(F32)
    kept = jnp.sum(jnp.where(lane16 == clip_col, keep[...].astype(F32), 0.0), axis=1, keepdims=True)
    place = (token_at(iota((64, 1), 0)).astype(F32) - first) * 64.0

    def live(d):
        return jnp.where(place + jnp.asarray(d, jnp.int32).astype(F32) < kept, 1.0, 0.0)

    lane1 = iota((1, 128), 1)

    def pair_mask(c):
        now = jnp.sum(jnp.where(lane1 == 2 * c, clips, 0.0), axis=1, keepdims=True)
        was = jnp.sum(jnp.where(lane1 == 2 * c - 1, clips, 0.0), axis=1, keepdims=True)
        return jnp.where(jnp.logical_and(now == was, iota((1, 1), 0) + c > 0), 1.0, 0.0)

    mask0, mask1 = pair_mask(2 * m), pair_mask(2 * m + 1)

    for f in range(2):
        sl[f] = slope(cv[f]) * bm[...]
        pump(9 + f)

    arrive("ps")
    squeezed = get_sums(psl)
    excite = sigmoid(exact(mmt, squeezed * sigmoid(squeezed), sqoe[...]))
    other = pl.ds(pl.multiple_of(64 * (1 - k), 64), 64)
    gather = select(patch_place(iota((256, 256), 0)) == iota((256, 256), 1))
    for f in range(2):
        hidden = xs[1, f, 16:272, :].astype(F32) + ac[f] * excite[f : f + 1, :]
        taps = mm(gather, hidden.astype(BF))
        base = 4 * (1 - f)
        rest = jnp.zeros((64, 128), F32)
        for s in range(4):
            tail = taps[64 * s : 64 * s + 64, 128:256]
            by = 16 * (s + base)
            rest = rest + (tail if by == 0 else pltpu.roll(tail, by, 1))
        main = taps[:, 0:128].astype(BF)
        if f == 0:
            mine = pl.ds(pl.multiple_of(64 * k, 64), 64)
            p1[mine, 0:128] = rest.astype(BF)
            for s in range(4):
                p1[mine, 128 * (s + 1) : 128 * (s + 2)] = main[64 * s : 64 * s + 64]
            start(remote(p1.at[mine], p1.at[mine], e_sem.at[0], e_sem.at[1], sibling))
            coming["even"] = lambda: remote(p1.at[other], p1.at[other], e_sem.at[0], e_sem.at[1], sibling).wait_recv()
        else:
            obuf[:, 512:640] = rest.astype(BF)
            for s in range(4):
                obuf[:, 128 * s : 128 * (s + 1)] = main[64 * s : 64 * s + 64]

    def send_odd():
        @pl.when(k == 0)
        def _():
            p0[64:128, :] = obuf[...]
            remote(obuf, p0.at[64:128], o_s.at[0], o_r.at[1], sibling).start()

        @pl.when(k == 1)
        def _():
            remote(obuf, p0.at[0:64], o_s.at[0], o_r.at[0], chip(m + 1, 1)).start()
            remote(obuf, p0.at[0:64], o_s.at[1], o_r.at[0], chip(m + 1, 0)).start()

    def odd_sent():
        remote(obuf, p0.at[0:64], o_s.at[0], o_r.at[0], sibling).wait_send()

        @pl.when(k == 1)
        def _():
            remote(obuf, p0.at[0:64], o_s.at[1], o_r.at[0], sibling).wait_send()

    def odd_here():
        remote(obuf, p0.at[0:64], o_s.at[0], o_r.at[0], sibling).wait_recv()

        @pl.when(k == 1)
        def _():
            remote(obuf, p0.at[64:128], o_s.at[0], o_r.at[1], sibling).wait_recv()

    send_odd()
    leaving.append(odd_sent)
    coming["odd"] = odd_here

    local[4].wait()
    R.end()
    fta[...] = rall[:, :, 1024:1152].reshape(512, 128).astype(F32)
    for p in range(8):
        rrest[0:64, 128 * p : 128 * p + 128] = fta[pl.ds(p, 64, stride=8), :].astype(BF)
    rrest[64:128, :] = jnp.zeros((64, 1024), BF)
    arrive("cot")
    order = select(token_at(iota((64, 64), 0)) == iota((64, 64), 1))
    back = jnp.concatenate([mm(order, cotb[0]).astype(BF), mm(order, cotb[1]).astype(BF)], axis=0)
    alive = jnp.concatenate([live(2 * m), live(2 * m + 1)], axis=0)
    gap[:, :, 0:512] = (
        (mmt(back, rall[:, :, 0:1024].reshape(512, 1024)) * alive).astype(BF).reshape(8, 16, 512)
    )
    pump(11)
    gap[:, :, 512:640] = (mmt(back, rrest[...]) * alive).astype(BF).reshape(8, 16, 128)

    def scattered(parts, chunk, slots):
        total = parts[chunk].astype(F32)
        for d in range(1, NT):
            total = total + slots[lax.rem(t + d, NT)].astype(F32)
        return total

    coming["rg"] = exchange(lambda o: gap.at[decoder_chunk(o)], rsg, t, 1)
    pump(12)

    def put_rows(src, value, dst, which):
        for i in range(16):
            src[i] = value[i : i + 1, :]

        @pl.when(is_self == 1)
        def _():
            dst[row_slot] = src[row_slot]

        @pl.when(is_self == 0)
        def _():
            i = trade[0]
            remote(src.at[i], dst.at[row_slot], pair.at[which, 0], pair.at[which, 1], row_dev(i)).start()

        for i in trade[1:]:
            remote(src.at[i], dst.at[row_slot], pair.at[which, 0], pair.at[which, 1], row_dev(i)).start()

        def both(wait):
            @pl.when(is_self == 1)
            def _():
                wait(remote(src.at[0:15], dst.at[0:15], pair.at[which, 0], pair.at[which, 1], sibling))

            @pl.when(is_self == 0)
            def _():
                wait(remote(src, dst, pair.at[which, 0], pair.at[which, 1], sibling))

        leaving.append(lambda: both(lambda copy: copy.wait_send()))
        return lambda: both(lambda copy: copy.wait_recv())

    def get_rows(dst):
        return jnp.concatenate([dst[i] for i in range(16)], axis=0)

    arrive("rg")
    coming["ga"] = put_rows(gas, scattered(gap, decoder_chunk(t), rsg), gad, 3)
    arrive("even", "odd")
    S.end()
    fta[...] = sall[:, :, 1152:1280].reshape(512, 128).astype(F32)
    ftb[...] = sall[:, :, 1280:1408].reshape(512, 128).astype(F32)
    rest = jnp.zeros((64, 128), F32)
    for s in range(8):
        srest[0:64, SLOT[s] : SLOT[s] + 128] = fta[pl.ds(s, 64, stride=8), :].astype(BF)
        tail = ftb[pl.ds(s, 64, stride=8), :]
        rest = rest + (tail if s == 0 else pltpu.roll(tail, 16 * s, 1))
    srest[0:64, 512:640] = rest.astype(BF)
    srest[64:128, :] = jnp.zeros((64, 1152), BF)

    mask_col = jnp.concatenate(
        [jnp.broadcast_to(mask0, (64, 1)), jnp.broadcast_to(mask1, (64, 1))], axis=0
    )

    def pre_part(w0, w1):
        return mmt(p0[...], w0) * mask_col + mmt(p1[...], w1)

    prep[:, :, 0:512] = (
        pre_part(sall[:, :, 0:640].reshape(512, 640), sall[:, :, 512:1152].reshape(512, 640))
        .astype(BF)
        .reshape(8, 16, 512)
    )
    prep[:, :, 512:640] = pre_part(srest[:, 0:640], srest[:, 512:1152]).astype(BF).reshape(8, 16, 128)
    coming["rp"] = exchange(lambda o: prep.at[frame_chunk(o)], rsp, t, 2)

    arrive("rp")
    pre = scattered(prep, frame_chunk(t), rsp)
    pre_slope = slope(pre)
    arrive("ga")
    in_frames = frame_chunk(t)
    gpf[in_frames] = (get_rows(gad) * pre_slope).astype(BF)
    coming["gp"] = exchange(lambda o: gpf.at[in_frames], gpf, in_frames, 5)
    coming["aa"] = put_rows(acs, (pre * sigmoid(pre)).astype(BF).astype(F32), acd, 4)
    arrive("gp")
    grads = gpf[...].reshape(128, 640)
    gpt[...] = mm(grads[:, 0:512], sall[:, :, 0:1152].reshape(512, 1152)) + mm(grads[:, 512:640], srest[...])
    ges[...] = gpt[other, 512:1152].astype(BF)
    start(remote(ges, ger, ge_sem.at[0], ge_sem.at[1], sibling))
    coming["ge"] = remote(ges, ger, ge_sem.at[0], ge_sem.at[1], sibling).wait_recv
    gos[0] = (gpt[0:64, 0:640] * mask0).astype(BF)
    gos[1] = (gpt[64:128, 0:640] * mask1).astype(BF)
    start(remote(gos.at[0], gor.at[k], go_s.at[0], go_r.at[k], chip(m - 1, 1)))

    @pl.when(k == 1)
    def _():
        remote(gos.at[1], gor.at[1], go_s.at[1], go_r.at[1], sibling).start()

    @pl.when(k == 0)
    def _():
        gor[0] = gos[1]

    def grad_odd_sent():
        @pl.when(k == 1)
        def _():
            remote(gos.at[1], gor.at[1], go_s.at[1], go_r.at[1], sibling).wait_send()

    def grad_odd_here():
        remote(gos.at[0], gor.at[1], go_s.at[0], go_r.at[1], sibling).wait_recv()

        @pl.when(k == 1)
        def _():
            remote(gos.at[0], gor.at[0], go_s.at[0], go_r.at[0], sibling).wait_recv()

    leaving.append(grad_odd_sent)
    coming["go"] = grad_odd_here

    arrive("aa")
    in_decoder = decoder_chunk(t)
    acf[in_decoder] = get_rows(acd).astype(BF)
    coming["af"] = exchange(lambda o: acf.at[in_decoder], acf, in_decoder, 6)

    arrive("ge", "go")
    mine = pl.ds(pl.multiple_of(64 * k, 64), 64)
    even = gpt[mine, 512:1152] + ger[...].astype(F32)
    odd = gor[0].astype(F32) + gor[1].astype(F32)
    ungather = select(patch_place(iota((256, 256), 1)) == iota((256, 256), 0))
    narrow = iota((64, 128), 1) < 16
    for f in range(2):
        if f == 0:
            tile, mains, base = even[:, 0:128], even[:, 128:640], 4
        else:
            tile, mains, base = odd[:, 512:640], odd[:, 0:512], 0
        main = jnp.concatenate([mains[:, 128 * s : 128 * s + 128] for s in range(4)], axis=0)
        tails = []
        for s in range(4):
            by = (128 - 16 * (s + base)) % 128
            tails.append(jnp.where(narrow, tile if by == 0 else pltpu.roll(tile, by, 1), 0.0))
        taps = jnp.concatenate([main, jnp.concatenate(tails, axis=0)], axis=1)
        top = taps.astype(BF)
        bottom = (taps - top.astype(F32)).astype(BF)
        grad = (mm(ungather, top) + mm(ungather, bottom)) * bm[...]
        gh[f] = grad
        pbuf[f : f + 1, :] = jnp.sum(grad * ac[f], axis=0, keepdims=True)

    inner = pbuf[...] * excite * (1.0 - excite)
    coming["pq"] = put_sums(psl2, exact(mm, inner, sqoe[...]), 7)
    arrive("af")
    acts = acf[...].reshape(128, 640)
    part = mm(acts[:, 0:512], rall[:, :, 0:1024].reshape(512, 1024)) + mm(acts[:, 512:640], rrest[...])
    low, high = part[0:64], part[64:128]
    kf = k.astype(F32)
    tks[...] = (low * kf + high * (1.0 - kf)).astype(BF)
    start(remote(tks, tkr, tk_sem.at[0], tk_sem.at[1], sibling))
    own_tokens = low * (1.0 - kf) + high * kf
    coming["tk"] = remote(tks, tkr, tk_sem.at[0], tk_sem.at[1], sibling).wait_recv

    arrive("pq")
    grad_squeezed = get_sums(psl2) * slope(squeezed)
    grad_pooled = exact(mmt, grad_squeezed, sqie[...]) * (1.0 / 196.0)
    outof = select(padded_place(iota((196, 256), 0)) == iota((196, 256), 1))
    for f in range(2):
        grad_active = gh[f] * excite[f : f + 1, :] + grad_pooled[f : f + 1, :]
        put_shifts(f, grad_active * sl[f])
    both = gh[...].reshape(512, 256)
    for dy in range(3):
        for dx in range(3):
            window = xs[2 - dx, :, 16 * (2 - dy) : 16 * (2 - dy) + 256, :].reshape(512, 256)
            both = both + mm(window, wc[3 * dy + dx])
    for f in range(2):
        turned = both[256 * f : 256 * f + 256].T[0:144].astype(BF)
        gout[f] = mmt(turned, outof).astype(BF)

    arrive("tk")
    rows = ((own_tokens + tkr[...].astype(F32)) * live(ctx)).astype(BF)
    llm[...] = mm(select(token_at(iota((64, 64), 1)) == iota((64, 64), 0)), rows).astype(BF)
    finish()


def per_device(features, group_kernel, squeeze_in, squeeze_out, sampler_kernel, readout_kernel, frame_clip, clip_keep, token_cotangent):
    V = pltpu.VMEM
    dma = pltpu.SemaphoreType.DMA
    scratch = [
        V((2, 144, 196), BF),
        V((9, 48, 144), BF),
        V((144, 144), BF),
        V((18, 1024), BF),
        V((32, 16, 1408), BF),
        V((32, 16, 1152), BF),
        V((128, 1152), BF),
        V((128, 1024), BF),
        V((512, 128), F32),
        V((512, 128), F32),
        V((2, 64, 1024), BF),
        V((9, 256, 256), BF),
        V((3, 2, 288, 256), BF),
        V((2, 256, 256), F32),
        V((2, 256, 256), F32),
        V((2, 256, 256), F32),
        V((256, 256), F32),
        V((2, 256, 256), F32),
        V((256, 288), BF),
        V((256, 288), BF),
        V((8, 256), F32),
        V((NT, 1, 768), F32),
        V((NT, 1, 768), F32),
        V((128, 640), BF),
        V((128, 640), BF),
        V((64, 640), BF),
        V((8, 16, 640), BF),
        V((8, 16, 640), BF),
        V((8, 16, 640), BF),
        V((8, 16, 640), BF),
        V((16, 1, 640), F32),
        V((16, 1, 640), F32),
        V((16, 1, 640), F32),
        V((16, 1, 640), F32),
        V((8, 16, 640), BF),
        V((8, 16, 640), BF),
        V((128, 1152), F32),
        V((64, 640), BF),
        V((64, 640), BF),
        V((2, 64, 640), BF),
        V((2, 64, 640), BF),
        V((64, 1024), BF),
        V((64, 1024), BF),
        dma((7,)),
        dma((2,)),
        dma((1,)), dma((32,)),
        dma((1,)), dma((32,)),
        dma((8, 2)),
        dma((2,)),
        dma((2,)), dma((2,)),
        dma((2,)),
        dma((2,)), dma((2,)),
        dma((2,)),
    ]
    spec = pl.BlockSpec(memory_space=pltpu.VMEM)
    hbm = pl.BlockSpec(memory_space=pltpu.HBM)
    llm_tokens, grad_features = pl.pallas_call(
        kernel,
        out_shape=(jax.ShapeDtypeStruct((64, 1024), BF), jax.ShapeDtypeStruct((2, 144, 196), BF)),
        in_specs=[hbm] * 6 + [spec] * 2 + [hbm],
        out_specs=(spec, spec),
        scratch_shapes=scratch,
        compiler_params=pltpu.CompilerParams(
            collective_id=0, has_side_effects=True, vmem_limit_bytes=62 * 1024 * 1024
        ),
        cost_estimate=pl.CostEstimate(flops=3_000_000_000, bytes_accessed=1_000_000, transcendentals=1_000_000),
        name="connector",
    )(
        features.transpose(0, 2, 1),
        group_kernel.transpose(0, 2, 1),
        squeeze_in,
        squeeze_out.T,
        sampler_kernel.reshape(144, 144),
        readout_kernel,
        frame_clip.reshape(1, 128),
        clip_keep.reshape(1, 16),
        token_cotangent,
    )
    return llm_tokens, grad_features.transpose(0, 2, 1)


def solution(mesh):
    placed = (
        P("ctx", None, "tp"),
        P(None, "tp", None),
        P("tp", None),
        P(None, "tp"),
        P("ctx", None, "tp"),
        P("ctx", "tp"),
        P(),
        P(),
        P("ctx", "tp"),
    )
    return jax.shard_map(
        per_device,
        mesh=mesh,
        in_specs=placed,
        out_specs=(P("ctx", "tp"), P("ctx", None, "tp")),
        check_vma=False,
    )
```

time: 81.8 us -> 75.5 us (0.923)
  the two profiles are of different devices: /device:TPU:4 before, /device:TPU:1 now
where the time goes in v2:
time: 75.5 us; the launch traced here: 75.4 us
  Pallas kernels  72.4 us (96%)
  local copies, waits for them, and re-layouts  2.27 us (3%)
    pallas_call x1, Pallas kernels, per_device(): pl.pallas_call(kernel, out_shape=(jax.ShapeDtypeStruct((64, 1024), BF), j...  72.4 us
    unnamed x4, local copies, waits for them, and re-layouts  2.27 us

profile of v2, /device:TPU:1, one launch (start us, length us, event | category | flops | bytes accessed | tf_op | source)
XLA Modules:
  0.0 75.4 jit_solution(8135955625005848361)
XLA Ops:
  0.6 72.4 %connector.1 = (bf16[64,1024]{1,0:T(8,128)(2,1)}, bf16[2,144,196]{2,1,0:T(8,128)(2,1)}) custom-call(bf16[2,144,196]{2,1,0:T(8,128)(2,1)} %bitcast.9, bf16[9,48,144]{2,1,0:T(8,128)(2,1)} %bitcast.8, bf16[144,288]{1,0:T(8,128)(2,1)} %sqi_h.1, bf16[144,288]{1,0:T(8,128)(2,1)} %bitcast.10, bf16[144,144]{1,0:T(8,128)(2,1)} %bitcast.11, bf16[18,1024]{1,0:T(8,128)(2,1)} %read_h.1, ...), custom_call_target="tpu_custom_call" | custom-call | flops 3000000000 | bytes 1000000 | tf_op jit(solution)/shard_map/connector/pallas_call | solution.py:743
  73.1 0.0 copy-start
  73.1 1.6 %copy.13 = bf16[64,1024]{1,0:T(8,128)(2,1)} copy(bf16[64,1024]{1,0:T(8,128)(2,1)} %get-tuple-element.8) | data formatting | bytes 262144
  74.7 0.0 copy-done
  74.7 0.7 copy.14
Async XLA Ops:
  73.1 1.6 %copy-start = (bf16[2,144,196]{2,1,0:T(8,128)(2,1)S(1)}, bf16[2,144,196]{2,1,0:T(8,128)(2,1)}, u32[]{:S(2)}) copy-start(bf16[2,144,196]{2,1,0:T(8,128)(2,1)} %get-tuple-element.5) | copy-start | bytes 338692

commit v3 on v2

--- a/solution.py
+++ b/solution.py
@@ -117,7 +117,7 @@
         )
 
     def exchange(source, slots, slot, which):
-        for d in range(1, NT):
+        for d in (4, 3, 5, 2, 6, 1, 7):
             o = lax.rem(t + d, NT)
             remote(source(o), slots.at[slot], pair.at[which, 0], pair.at[which, 1], tdev(d)).start()
         all_of = remote(slots.at[0 : NT - 1], slots.at[0 : NT - 1], pair.at[which, 0], pair.at[which, 1], tdev(1))
@@ -310,32 +310,32 @@
         cores(
             [
                 lambda: (R.a_start(), S.a_start()),
-                lambda: (R.a_z(1), R.a_z(3)),
-                lambda: (R.a_z(2), R.a_ring(1, 0)),
-                lambda: R.a_ring(1, 1, 3),
-                lambda: (R.a_ring(1, 2), R.a_ring(2, 0), S.a_z(1), S.a_z(3)),
-                lambda: R.a_ring(2, 1, 3),
-                lambda: (R.a_ring(2, 2), R.a_ring(3, 0), S.a_z(2)),
-                lambda: (R.a_ring(3, 1, 3, 2), S.a_ring(1, 0)),
-                lambda: S.a_ring(1, 1, 3, 2),
-                lambda: S.a_ring(2, 0, 1),
-                lambda: S.a_ring(2, 3, 2),
-                lambda: S.a_ring(3, 0, 1),
-                lambda: S.a_ring(3, 3, 2),
+                lambda: (R.a_z(1), R.a_z(3), R.a_z(2)),
+                lambda: (R.a_ring(1, 0), S.a_z(1), S.a_z(3)),
+                lambda: (R.a_ring(1, 1, 3, 2), S.a_z(2)),
+                lambda: (R.a_ring(2, 0), S.a_ring(1, 0)),
+                lambda: (R.a_ring(2, 1, 3, 2), S.a_ring(1, 1)),
+                lambda: (R.a_ring(3, 0), S.a_ring(1, 3, 2)),
+                lambda: (R.a_ring(3, 1, 3, 2), S.a_ring(2, 0)),
+                lambda: S.a_ring(2, 1, 3),
+                lambda: S.a_ring(2, 2),
+                lambda: S.a_ring(3, 0),
+                lambda: S.a_ring(3, 1, 3),
+                lambda: S.a_ring(3, 2),
             ][n],
             [
                 lambda: (R.b_start(), S.b_start()),
                 lambda: R.b_ring(1),
-                lambda: (R.b_ring(2), R.b_pass(0)),
-                lambda: (R.b_ring(3), S.b_ring(1)),
-                lambda: (R.b_ring(4), R.b_pass(1, -1)),
-                lambda: (R.b_pass(2, -2), S.b_ring(2)),
-                lambda: (R.b_pass(3, -3, 4), S.b_ring(3), S.b_pass(0)),
-                lambda: S.b_ring(4),
-                lambda: S.b_pass(1, -1),
-                lambda: S.b_pass(2, -2),
-                lambda: S.b_pass(3, -3),
-                lambda: S.b_pass(4),
+                lambda: (R.b_ring(2), S.b_ring(1)),
+                lambda: (R.b_ring(3), R.b_pass(0)),
+                lambda: (S.b_ring(2), R.b_ring(4), R.b_pass(1, -1)),
+                lambda: (R.b_pass(2, -2), S.b_pass(0)),
+                lambda: (R.b_pass(3, -3, 4), S.b_ring(3)),
+                lambda: (S.b_pass(1, -1), S.b_ring(4)),
+                lambda: S.b_pass(2),
+                lambda: S.b_pass(-2),
+                lambda: S.b_pass(3),
+                lambda: S.b_pass(-3, 4),
                 lambda: None,
             ][n],
         )
@@ -530,7 +530,7 @@
             i = trade[0]
             remote(src.at[i], dst.at[row_slot], pair.at[which, 0], pair.at[which, 1], row_dev(i)).start()
 
-        for i in trade[1:]:
+        for i in [trade[j] for j in (10, 6, 14, 2, 9, 11, 5, 7, 13, 15, 1, 3, 8, 4, 12)]:
             remote(src.at[i], dst.at[row_slot], pair.at[which, 0], pair.at[which, 1], row_dev(i)).start()
 
         def both(wait):
@@ -548,8 +548,6 @@
     def get_rows(dst):
         return jnp.concatenate([dst[i] for i in range(16)], axis=0)
 
-    arrive("rg")
-    coming["ga"] = put_rows(gas, scattered(gap, decoder_chunk(t), rsg), gad, 3)
     arrive("even", "odd")
     S.end()
     fta[...] = sall[:, :, 1152:1280].reshape(512, 128).astype(F32)
@@ -577,6 +575,8 @@
     prep[:, :, 512:640] = pre_part(srest[:, 0:640], srest[:, 512:1152]).astype(BF).reshape(8, 16, 128)
     coming["rp"] = exchange(lambda o: prep.at[frame_chunk(o)], rsp, t, 2)
 
+    arrive("rg")
+    coming["ga"] = put_rows(gas, scattered(gap, decoder_chunk(t), rsg), gad, 3)
     arrive("rp")
     pre = scattered(prep, frame_chunk(t), rsp)
     pre_slope = slope(pre)
@@ -587,13 +587,13 @@
     coming["aa"] = put_rows(acs, (pre * sigmoid(pre)).astype(BF).astype(F32), acd, 4)
     arrive("gp")
     grads = gpf[...].reshape(128, 640)
-    gpt[...] = mm(grads[:, 0:512], sall[:, :, 0:1152].reshape(512, 1152)) + mm(grads[:, 512:640], srest[...])
-    ges[...] = gpt[other, 512:1152].astype(BF)
-    start(remote(ges, ger, ge_sem.at[0], ge_sem.at[1], sibling))
-    coming["ge"] = remote(ges, ger, ge_sem.at[0], ge_sem.at[1], sibling).wait_recv
+    def grad_taps(lanes):
+        gpt[:, lanes] = mm(grads[:, 0:512], sall[:, :, lanes].reshape(512, lanes.stop - lanes.start)) + mm(grads[:, 512:640], srest[:, lanes])
+
+    grad_taps(slice(0, 640))
     gos[0] = (gpt[0:64, 0:640] * mask0).astype(BF)
+    start(remote(gos.at[0], gor.at[k], go_s.at[0], go_r.at[k], chip(m - 1, 1)))
     gos[1] = (gpt[64:128, 0:640] * mask1).astype(BF)
-    start(remote(gos.at[0], gor.at[k], go_s.at[0], go_r.at[k], chip(m - 1, 1)))
 
     @pl.when(k == 1)
     def _():
@@ -616,6 +616,10 @@
             remote(gos.at[0], gor.at[0], go_s.at[0], go_r.at[0], sibling).wait_recv()
 
     leaving.append(grad_odd_sent)
+    grad_taps(slice(640, 1152))
+    ges[...] = gpt[other, 512:1152].astype(BF)
+    start(remote(ges, ger, ge_sem.at[0], ge_sem.at[1], sibling))
+    coming["ge"] = remote(ges, ger, ge_sem.at[0], ge_sem.at[1], sibling).wait_recv
     coming["go"] = grad_odd_here
 
     arrive("aa")

time: 75.5 us -> 71.2 us (0.943)
  Pallas kernels: 72.4 us -> 68.1 us
    pallas_call x1, Pallas kernels: 72.4 us -> 68.1 us  [per_device(): pl.pallas_call(kernel, out_shape=(jax.ShapeDtypeStruct((64, 1024), BF), j...]
where the time goes in v3:
time: 71.2 us; the launch traced here: 71 us
  Pallas kernels  68.1 us (96%)
  local copies, waits for them, and re-layouts  2.27 us (3%)
    pallas_call x1, Pallas kernels, per_device(): pl.pallas_call(kernel, out_shape=(jax.ShapeDtypeStruct((64, 1024), BF), j...  68.1 us
    unnamed x4, local copies, waits for them, and re-layouts  2.27 us

profile of v3, /device:TPU:1, one launch (start us, length us, event | category | flops | bytes accessed | tf_op | source)
XLA Modules:
  0.0 71.0 jit_solution(3605236285464089323)
XLA Ops:
  0.6 68.1 %connector.1 = (bf16[64,1024]{1,0:T(8,128)(2,1)}, bf16[2,144,196]{2,1,0:T(8,128)(2,1)}) custom-call(bf16[2,144,196]{2,1,0:T(8,128)(2,1)} %bitcast.9, bf16[9,48,144]{2,1,0:T(8,128)(2,1)} %bitcast.8, bf16[144,288]{1,0:T(8,128)(2,1)} %sqi_h.1, bf16[144,288]{1,0:T(8,128)(2,1)} %bitcast.10, bf16[144,144]{1,0:T(8,128)(2,1)} %bitcast.11, bf16[18,1024]{1,0:T(8,128)(2,1)} %read_h.1, ...), custom_call_target="tpu_custom_call" | custom-call | flops 3000000000 | bytes 1000000 | tf_op jit(solution)/shard_map/connector/pallas_call | solution.py:747
  68.8 0.0 copy-start
  68.8 1.6 %copy.13 = bf16[64,1024]{1,0:T(8,128)(2,1)} copy(bf16[64,1024]{1,0:T(8,128)(2,1)} %get-tuple-element.8) | data formatting | bytes 262144
  70.4 0.0 copy-done
  70.4 0.7 copy.14
Async XLA Ops:
  68.8 1.6 %copy-start = (bf16[2,144,196]{2,1,0:T(8,128)(2,1)S(1)}, bf16[2,144,196]{2,1,0:T(8,128)(2,1)}, u32[]{:S(2)}) copy-start(bf16[2,144,196]{2,1,0:T(8,128)(2,1)} %get-tuple-element.5) | copy-start | bytes 338692

commit v4 on v3

--- a/solution.py
+++ b/solution.py
@@ -155,13 +155,21 @@
         local.append(pltpu.make_async_copy(src, dst, load.at[i]))
         local[-1].start()
 
-    hello(sibling)
-    for d in range(1, NX):
+    trade = [lax.rem(row_slot + j, 16) for j in range(16)]
+
+    @pl.when(is_self == 0)
+    def _():
+        hello(row_dev(trade[0]))
+
+    for j in (10, 6, 14, 2, 9, 11, 5, 7, 13, 15, 1, 3, 8, 4, 12):
+        hello(row_dev(trade[j]))
+    for d in (4, 3, 5, 2, 6, 1, 7):
+        hello(tdev(d))
+    for d in (2, 1, 3):
         hello(xdev(d))
     hello(zdev(1))
     hello(zdev(-1))
-    for d in range(1, NT):
-        hello(tdev(d))
+    hello(sibling)
     hello(chip(m - 1, 1))
 
     @pl.when(k == 1)
@@ -169,14 +177,6 @@
         hello(chip(m + 1, 0))
         hello(chip(m + 1, 1))
 
-    trade = [lax.rem(row_slot + j, 16) for j in range(16)]
-
-    @pl.when(is_self == 0)
-    def _():
-        hello(row_dev(trade[0]))
-
-    for j in range(1, 16):
-        hello(row_dev(trade[j]))
 
     own = 4 * z + x
     local[0].wait()
@@ -230,7 +230,7 @@
             self.send(0, e, 4 + 7 * e + hop(1), zdev(-1))
 
         def a_start(self):
-            for e in (1, 3, 2):
+            for e in (2, 1, 3):
                 self.send(0, 0, (-e) % 4, xdev(e))
             self.a_z(0)
 
@@ -627,11 +627,11 @@
     acf[in_decoder] = get_rows(acd).astype(BF)
     coming["af"] = exchange(lambda o: acf.at[in_decoder], acf, in_decoder, 6)
 
+    ungather = select(patch_place(iota((256, 256), 1)) == iota((256, 256), 0))
     arrive("ge", "go")
     mine = pl.ds(pl.multiple_of(64 * k, 64), 64)
     even = gpt[mine, 512:1152] + ger[...].astype(F32)
     odd = gor[0].astype(F32) + gor[1].astype(F32)
-    ungather = select(patch_place(iota((256, 256), 1)) == iota((256, 256), 0))
     narrow = iota((64, 128), 1) < 16
     for f in range(2):
         if f == 0:
@@ -662,10 +662,12 @@
     own_tokens = low * (1.0 - kf) + high * kf
     coming["tk"] = remote(tks, tkr, tk_sem.at[0], tk_sem.at[1], sibling).wait_recv
 
+    outof = select(padded_place(iota((196, 256), 0)) == iota((196, 256), 1))
+    natural = select(token_at(iota((64, 64), 1)) == iota((64, 64), 0))
+    squeezed_slope = slope(squeezed)
     arrive("pq")
-    grad_squeezed = get_sums(psl2) * slope(squeezed)
+    grad_squeezed = get_sums(psl2) * squeezed_slope
     grad_pooled = exact(mmt, grad_squeezed, sqie[...]) * (1.0 / 196.0)
-    outof = select(padded_place(iota((196, 256), 0)) == iota((196, 256), 1))
     for f in range(2):
         grad_active = gh[f] * excite[f : f + 1, :] + grad_pooled[f : f + 1, :]
         put_shifts(f, grad_active * sl[f])
@@ -680,7 +682,7 @@
 
     arrive("tk")
     rows = ((own_tokens + tkr[...].astype(F32)) * live(ctx)).astype(BF)
-    llm[...] = mm(select(token_at(iota((64, 64), 1)) == iota((64, 64), 0)), rows).astype(BF)
+    llm[...] = mm(natural, rows).astype(BF)
     finish()
 
 

time: 71.2 us -> 70.9 us (level)
  no operation moved by 1% of the time
where the time goes in v4:
time: 70.9 us; the launch traced here: 70.7 us
  Pallas kernels  67.8 us (96%)
  local copies, waits for them, and re-layouts  2.27 us (3%)
    pallas_call x1, Pallas kernels, per_device(): pl.pallas_call(kernel, out_shape=(jax.ShapeDtypeStruct((64, 1024), BF), j...  67.8 us
    unnamed x4, local copies, waits for them, and re-layouts  2.27 us

profile of v4, /device:TPU:1, one launch (start us, length us, event | category | flops | bytes accessed | tf_op | source)
XLA Modules:
  0.0 70.7 jit_solution(6045179399539834489)
XLA Ops:
  0.6 67.8 %connector.1 = (bf16[64,1024]{1,0:T(8,128)(2,1)}, bf16[2,144,196]{2,1,0:T(8,128)(2,1)}) custom-call(bf16[2,144,196]{2,1,0:T(8,128)(2,1)} %bitcast.9, bf16[9,48,144]{2,1,0:T(8,128)(2,1)} %bitcast.8, bf16[144,288]{1,0:T(8,128)(2,1)} %sqi_h.1, bf16[144,288]{1,0:T(8,128)(2,1)} %bitcast.10, bf16[144,144]{1,0:T(8,128)(2,1)} %bitcast.11, bf16[18,1024]{1,0:T(8,128)(2,1)} %read_h.1, ...), custom_call_target="tpu_custom_call" | custom-call | flops 3000000000 | bytes 1000000 | tf_op jit(solution)/shard_map/connector/pallas_call | solution.py:749
  68.5 0.0 copy-start
  68.5 1.6 %copy.13 = bf16[64,1024]{1,0:T(8,128)(2,1)} copy(bf16[64,1024]{1,0:T(8,128)(2,1)} %get-tuple-element.8) | data formatting | bytes 262144
  70.1 0.0 copy-done
  70.1 0.7 copy.14
Async XLA Ops:
  68.5 1.6 %copy-start = (bf16[2,144,196]{2,1,0:T(8,128)(2,1)S(1)}, bf16[2,144,196]{2,1,0:T(8,128)(2,1)}, u32[]{:S(2)}) copy-start(bf16[2,144,196]{2,1,0:T(8,128)(2,1)} %get-tuple-element.5) | copy-start | bytes 338692

commit v5 on v4

--- a/solution.py
+++ b/solution.py
@@ -506,6 +506,7 @@
         (mmt(back, rall[:, :, 0:1024].reshape(512, 1024)) * alive).astype(BF).reshape(8, 16, 512)
     )
     pump(11)
+    pump(12)
     gap[:, :, 512:640] = (mmt(back, rrest[...]) * alive).astype(BF).reshape(8, 16, 128)
 
     def scattered(parts, chunk, slots):
@@ -515,7 +516,6 @@
         return total
 
     coming["rg"] = exchange(lambda o: gap.at[decoder_chunk(o)], rsg, t, 1)
-    pump(12)
 
     def put_rows(src, value, dst, which):
         for i in range(16):
@@ -572,8 +572,10 @@
         .astype(BF)
         .reshape(8, 16, 512)
     )
+    main_here = exchange(lambda o: prep.at[frame_chunk(o), :, 0:512], rsp.at[:, :, 0:512], t, 2)
     prep[:, :, 512:640] = pre_part(srest[:, 0:640], srest[:, 512:1152]).astype(BF).reshape(8, 16, 128)
-    coming["rp"] = exchange(lambda o: prep.at[frame_chunk(o)], rsp, t, 2)
+    tail_here = exchange(lambda o: prep.at[frame_chunk(o), :, 512:640], rsp.at[:, :, 512:640], t, 8)
+    coming["rp"] = lambda: (main_here(), tail_here())
 
     arrive("rg")
     coming["ga"] = put_rows(gas, scattered(gap, decoder_chunk(t), rsg), gad, 3)
@@ -737,7 +739,7 @@
         dma((2,)),
         dma((1,)), dma((32,)),
         dma((1,)), dma((32,)),
-        dma((8, 2)),
+        dma((9, 2)),
         dma((2,)),
         dma((2,)), dma((2,)),
         dma((2,)),

time: 70.9 us -> 70.8 us (level)
  no operation moved by 1% of the time
where the time goes in v5:
time: 70.8 us; the launch traced here: 70.7 us
  Pallas kernels  67.8 us (96%)
  local copies, waits for them, and re-layouts  2.27 us (3%)
    pallas_call x1, Pallas kernels, per_device(): pl.pallas_call(kernel, out_shape=(jax.ShapeDtypeStruct((64, 1024), BF), j...  67.8 us
    unnamed x4, local copies, waits for them, and re-layouts  2.27 us

profile of v5, /device:TPU:1, one launch (start us, length us, event | category | flops | bytes accessed | tf_op | source)
XLA Modules:
  0.0 70.7 jit_solution(16110452807264667774)
XLA Ops:
  0.6 67.8 %connector.1 = (bf16[64,1024]{1,0:T(8,128)(2,1)}, bf16[2,144,196]{2,1,0:T(8,128)(2,1)}) custom-call(bf16[2,144,196]{2,1,0:T(8,128)(2,1)} %bitcast.9, bf16[9,48,144]{2,1,0:T(8,128)(2,1)} %bitcast.8, bf16[144,288]{1,0:T(8,128)(2,1)} %sqi_h.1, bf16[144,288]{1,0:T(8,128)(2,1)} %bitcast.10, bf16[144,144]{1,0:T(8,128)(2,1)} %bitcast.11, bf16[18,1024]{1,0:T(8,128)(2,1)} %read_h.1, ...), custom_call_target="tpu_custom_call" | custom-call | flops 3000000000 | bytes 1000000 | tf_op jit(solution)/shard_map/connector/pallas_call | solution.py:751
  68.4 0.0 copy-start
  68.4 1.6 %copy.13 = bf16[64,1024]{1,0:T(8,128)(2,1)} copy(bf16[64,1024]{1,0:T(8,128)(2,1)} %get-tuple-element.8) | data formatting | bytes 262144
  70.0 0.0 copy-done
  70.0 0.7 copy.14
Async XLA Ops:
  68.4 1.6 %copy-start = (bf16[2,144,196]{2,1,0:T(8,128)(2,1)S(1)}, bf16[2,144,196]{2,1,0:T(8,128)(2,1)}, u32[]{:S(2)}) copy-start(bf16[2,144,196]{2,1,0:T(8,128)(2,1)} %get-tuple-element.5) | copy-start | bytes 338692
